TPU v7x, 32 devices: a whole 2x2x4 slice. The times are simulated.
32 devices in a mesh: grp: 2 (over y), dev: 4 (over z), tp: 4 (over x, core).
Axes of the slice: x: 2, y: 2, z: 4, core: 2. Of those that a mesh axis runs over, the one named last changes fastest.
Arguments:
- passage_hidden: bfloat16 [8192, 3584], P(('grp', 'dev', 'tp')), parts along dimension 0, may hold values from -6 to 6
- query_hidden: bfloat16 [1024, 3584], P(('grp', 'dev', 'tp')), parts along dimension 0, may hold values from -6 to 6
- gain_in: bfloat16 [3584], replicated, may hold values from 0.5 to 1.5
- gain_out: bfloat16 [3584], replicated, may hold values from 0.5 to 1.5
- w_query: bfloat16 [3584, 4096], P(None, 'tp'), may hold values from -2 to 2
- w_key: bfloat16 [3584, 2048], P(None, 'tp'), may hold values from -2 to 2
- w_value: bfloat16 [3584, 2048], P(None, 'tp'), may hold values from -0.09375 to 0.09375
- w_out: bfloat16 [4096, 3584], P('tp'), may hold values from -0.09375 to 0.09375
- pair_passage: int32 [16], P(('grp', 'dev')), parts along dimension 0, may hold values from 0 to 7, as said below
- pair_count: int32 [8], P(('grp', 'dev')), parts along dimension 0, may hold values from 1 to 2, 6 in all
Outputs:
- layer_out: bfloat16 [1024, 3584], P(('grp', 'dev', 'tp')), parts along dimension 0
There are 2 independent parts, one for each index of `grp`. A program takes and returns all parts, laid end to end along the dimension named above; an argument that names none is the same for every part. Nothing has to cross between parts.
Inputs may be any that keep to these rules, and one draw needn't show every extreme that they name: `pair_passage`: pair slot j belongs to owner floor(j / 2). Document owner k holds the ids k * 2 to (k + 1) * 2 - 1; the 2 slots of one owner name passages of 2 different document owners. Document owners with low k are named more often. Owner o's live pairs are its first pair_count[o] slots; the counts sum to 6.
All inputs are finite; a program needn't handle non-finite values. No bound on the sum of `pair_count` on one device may be relied on, other than what follows from the above.
Results may differ from a plain program's by a relative error of at most 0.012.
The roundings to bfloat16 on the way count: a program that leaves them out, or rounds other values in their place, can miss the bound.
Values may be sent and summed in bfloat16 or wider, within the bound.
A program may use at most 128 MiB of HBM per device.

v0:
```python
import math

import jax
import jax.numpy as jnp
from jax import lax
from jax.sharding import PartitionSpec as P

HD = 256
PLEN = 512
QLEN = 64


epsilon = 1e-06
softcap_limit = 50.0


def settle(values):
    return lax.optimization_barrier(values.astype(jnp.bfloat16)).astype(jnp.float32)


def capped(scores):
    return softcap_limit * jnp.tanh(scores / softcap_limit)


def normalize(rows, gain):
    values = rows.astype(jnp.float32)
    inverse_rms = lax.rsqrt(jnp.mean(values * values, axis=-1, keepdims=True) + epsilon)
    return (values * inverse_rms * gain.astype(jnp.float32)).astype(jnp.bfloat16)


def rotate(values, positions):
    head_width = values.shape[-1]
    half_width = head_width // 2
    frequency = 10000.0 ** (-2.0 * jnp.arange(half_width, dtype=jnp.float32) / head_width)
    angles = positions.astype(jnp.float32)[:, None] * frequency[None, :]
    cosine = jnp.cos(angles)[:, None, :]
    sine = jnp.sin(angles)[:, None, :]
    lower_half = values[..., :half_width]
    upper_half = values[..., half_width:]
    return jnp.concatenate(
        [lower_half * cosine - upper_half * sine, upper_half * cosine + lower_half * sine], axis=-1
    )


def attend(query_rows, keys_own, values_own, far_block):
    heads_kv = keys_own.shape[1]
    head_width = keys_own.shape[2]
    keys_far = far_block[:, : heads_kv * head_width].reshape(-1, heads_kv, head_width)
    values_far = far_block[:, heads_kv * head_width :].reshape(-1, heads_kv, head_width)
    far_scores = jnp.einsum(
        "qkgd,pkd->kgqp", query_rows, keys_far, preferred_element_type=jnp.float32
    )
    near_scores = jnp.einsum(
        "qkgd,tkd->kgqt", query_rows, keys_own, preferred_element_type=jnp.float32
    )
    suffix_len = query_rows.shape[0]
    causal = jnp.arange(suffix_len)[:, None] >= jnp.arange(suffix_len)[None, :]
    far_weight = jnp.exp(capped(far_scores))
    near_weight = jnp.where(causal, jnp.exp(capped(near_scores)), 0.0)
    denominator = jnp.sum(far_weight, axis=-1, keepdims=True) + jnp.sum(
        near_weight, axis=-1, keepdims=True
    )
    far_prob = (far_weight / denominator).astype(jnp.bfloat16)
    near_prob = (near_weight / denominator).astype(jnp.bfloat16)
    combined = jnp.einsum(
        "kgqp,pkd->qkgd", far_prob, values_far, preferred_element_type=jnp.float32
    )
    combined = combined + jnp.einsum(
        "kgqt,tkd->qkgd", near_prob, values_own, preferred_element_type=jnp.float32
    )
    return combined.astype(jnp.bfloat16).reshape(suffix_len, -1)


def shards(
    passage_hidden,
    query_hidden,
    gain_in,
    gain_out,
    w_query,
    w_key,
    w_value,
    w_out,
    pair_passage,
    pair_count,
):
    kv_width = w_key.shape[1]
    heads_kv = kv_width // HD
    heads_q = w_query.shape[1] // HD
    groups = heads_q // heads_kv
    pair_slots = pair_passage.shape[0]
    segment = lax.all_gather(passage_hidden, "tp", axis=0, tiled=True)
    normed = normalize(segment, gain_in)
    positions = jnp.arange(segment.shape[0]) % PLEN
    raw_keys = jnp.dot(normed, w_key, preferred_element_type=jnp.float32).reshape(-1, heads_kv, HD)
    rotated_keys = rotate(raw_keys, positions).reshape(-1, kv_width)
    values = jnp.dot(normed, w_value, preferred_element_type=jnp.float32)
    prepared = jnp.concatenate([rotated_keys, values], axis=1).astype(jnp.bfloat16)
    prepared = prepared.reshape(-1, PLEN, 2 * kv_width)
    segment = lax.all_gather(query_hidden, "tp", axis=0, tiled=True)
    normed = normalize(segment, gain_in)
    positions = PLEN + jnp.arange(segment.shape[0]) % QLEN
    raw_queries = jnp.dot(normed, w_query, preferred_element_type=jnp.float32).reshape(
        -1, heads_q, HD
    )
    rotated_queries = (rotate(raw_queries, positions) * HD ** (-0.5)).reshape(-1, heads_q * HD)
    raw_keys = jnp.dot(normed, w_key, preferred_element_type=jnp.float32).reshape(-1, heads_kv, HD)
    rotated_keys = rotate(raw_keys, positions).reshape(-1, kv_width)
    values = jnp.dot(normed, w_value, preferred_element_type=jnp.float32)
    projected = jnp.concatenate([rotated_queries, rotated_keys, values], axis=1).astype(
        jnp.bfloat16
    )
    split_at = heads_q * HD
    queries = projected[:, :split_at].reshape(pair_slots, QLEN, heads_kv, groups, HD)
    own_keys = projected[:, split_at : split_at + kv_width].reshape(pair_slots, QLEN, heads_kv, HD)
    own_values = projected[:, split_at + kv_width :].reshape(pair_slots, QLEN, heads_kv, HD)
    bundle = math.gcd(pair_slots, 4)

    def grouped(values):
        return values.reshape((pair_slots // bundle, bundle) + values.shape[1:])

    fetched = lax.all_gather(prepared, "dev", axis=0, tiled=True)

    def one_pair(query_rows, keys_own, values_own, passage_row):
        far_block = lax.dynamic_index_in_dim(fetched, passage_row, 0, keepdims=False)
        return attend(query_rows, keys_own, values_own, far_block)

    def one_bundle(members):
        return jax.vmap(one_pair)(members[0], members[1], members[2], members[3])

    attended_rows = lax.map(
        one_bundle,
        (grouped(queries), grouped(own_keys), grouped(own_values), grouped(pair_passage)),
    )
    attended = attended_rows.reshape(pair_slots * QLEN, heads_q * HD)
    local_rows = query_hidden.shape[0]
    merged = lax.psum_scatter(
        settle(jnp.dot(attended, w_out, preferred_element_type=jnp.float32)).astype(jnp.bfloat16),
        "tp",
        scatter_dimension=0,
        tiled=True,
    ).astype(jnp.float32)
    inverse_rms = lax.rsqrt(jnp.mean(merged * merged, axis=-1, keepdims=True) + epsilon)
    branch = merged * inverse_rms * gain_out.astype(jnp.float32)
    row_ids = lax.axis_index("tp") * local_rows + jnp.arange(local_rows)
    alive = row_ids // QLEN < pair_count[0]
    layer_out = jnp.where(alive[:, None], query_hidden.astype(jnp.float32) + branch, 0.0)
    return layer_out.astype(jnp.bfloat16)


def solution(mesh):
    placed = (
        P(("grp", "dev", "tp"), None),
        P(("grp", "dev", "tp"), None),
        P(),
        P(),
        P(None, "tp"),
        P(None, "tp"),
        P(None, "tp"),
        P("tp", None),
        P(("grp", "dev")),
        P(("grp", "dev")),
    )
    return jax.shard_map(
        shards, mesh=mesh, in_specs=placed, out_specs=P(("grp", "dev", "tp"), None), check_vma=False
    )
```

profile of v0, /device:TPU:0, one launch (start us, length us, event | category | flops | bytes accessed | tf_op | source)
XLA Modules:
  0.0 287.3 jit_solution(7114056591272018217)
XLA Ops:
  6.5 0.0 all-gather.3.cloned.1.call-start
  6.5 0.7 all-gather.3.cloned.1.call-update
  7.3 0.0 all-gather.5.cloned.1.call-start
  7.3 0.7 convert_element_type.88
  8.0 1.9 multiply_cosine_fusion
  9.9 54.1 %all-gather.3.cloned.1.call-done = bf16[1024,3584]{1,0:T(8,128)(2,1)} async-done(((bf16[256,3584]{1,0:T(8,128)(2,1)}), bf16[1024,3584]{1,0:T(8,128)(2,1)}) %all-gather.3.cloned.1.call-update) | async-done | bytes 7340048 | tf_op jit(solution)/shard_map/all_gather | solution.py:91
  64.0 0.0 copy-start
  64.0 4.7 %fusion = f32[1024]{0:T(1024)S(1)} fusion(bf16[1024,3584]{1,0:T(8,128)(2,1)} %all-gather.3.cloned.1.call-done), kind=kLoop, calls=%fused_computation.3 | loop fusion | flops 11009024 | bytes 7344128 | tf_op jit(solution)/shard_map/reduce_sum | solution.py:27
  68.7 0.4 copy-done
  69.2 6.3 %fusion.5 = f32[1024,512]{0,1:T(8,128)S(1)} fusion(bf16[3584,512]{1,0:T(8,128)(2,1)} %param.15, bf16[1024,3584]{1,0:T(8,128)(2,1)S(1)} %copy-done, f32[3584]{0:T(1024)S(1)} %convert_element_type.88, f32[1024]{0:T(1024)S(1)} %add_rsqrt_fusion), kind=kOutput, calls=%fused_computation.10 | convolution fusion | flops 3772776448 | bytes 13125632 | tf_op jit(solution)/shard_map/dot_general | solution.py:94
  75.5 0.4 subtract_convert_fusion
  75.9 0.1 pad_maximum_fusion.1
  76.0 1.0 reshape.242
  76.9 1.5 copy.49
  78.4 8.1 %fusion.10 = bf16[1024,512]{1,0:T(8,128)(2,1)S(1)} fusion(bf16[3584,512]{1,0:T(8,128)(2,1)} %param.16, bf16[1024,3584]{1,0:T(8,128)(2,1)} %all-gather.3.cloned.1.call-done, f32[3584]{0:T(1024)S(1)} %convert_element_type.88, f32[1024]{0:T(1024)S(1)} %add_rsqrt_fusion), kind=kOutput, calls=%fused_computation.15 | convolution fusion | flops 3773300736 | bytes 12077056 | tf_op jit(solution)/shard_map/dot_general | solution.py:96
  86.5 0.0 copy-start.1
  86.5 1.7 pad_maximum_fusion
  88.2 0.0 all-gather.5.cloned.1.call-update
  88.2 0.0 reduce-scatter.2.cloned.1.call-start
  88.3 0.0 copy-done.1
  88.3 9.3 %all_gather.11 = bf16[128,3584]{1,0:T(8,128)(2,1)S(1)} all-gather(bf16[32,3584]{1,0:T(8,128)(2,1)S(1)} %copy-done.1), channel_id=1, replica_groups=mesh['grp'=2,'dev'=4,'tp'=4] {'tp'}, dimensions={0}, use_global_device_ids=true | all-gather | bytes 1146880 | tf_op jit(solution)/shard_map/all_gather | solution.py:99
  97.6 0.3 fusion.7
  97.9 4.8 %fusion.49 = f32[128,1024]{1,0:T(8,128)S(1)} fusion(bf16[3584,1024]{1,0:T(8,128)(2,1)} %param.14, bf16[128,3584]{1,0:T(8,128)(2,1)S(1)} %all_gather.11, f32[3584]{0:T(1024)S(1)} %convert_element_type.88, f32[128]{0:T(128)S(1)} %add_rsqrt_fusion.2), kind=kOutput, calls=%fused_computation.84 | convolution fusion | flops 941359104 | bytes 8796672 | tf_op jit(solution)/shard_map/dot_general | solution.py:102
  102.8 0.2 reshape.221
  103.0 2.7 fusion.47
  105.8 0.2 reshape.222
  105.9 0.0 copy-start.4
  106.0 2.7 convolution_convert_fusion.1
  108.8 0.3 multiply_cosine_fusion.1
  109.1 0.1 fusion.53
  109.3 0.1 fusion.52
  109.4 0.1 multiply_subtract_fusion
  109.5 0.0 copy-done.4
  109.5 0.0 copy-start.2
  109.5 0.7 copy-done.2
  110.2 1.0 fusion.55
  111.2 126.9 %all-gather.5.cloned.1.call-done = bf16[8,512,1024]{2,1,0:T(8,128)(2,1)} async-done(((bf16[2,512,1024]{2,1,0:T(8,128)(2,1)}), bf16[8,512,1024]{2,1,0:T(8,128)(2,1)}) %all-gather.5.cloned.1.call-update) | async-done | bytes 8388624 | tf_op jit(solution)/shard_map/all_gather | solution.py:121
  238.0 4.1 %gather_fusion = bf16[2,512,1024]{2,1,0:T(8,128)(2,1)S(1)} fusion(bf16[8,512,1024]{2,1,0:T(8,128)(2,1)} %all-gather.5.cloned.1.call-done, s32[2]{0:T(128)S(1)} %fusion.44), kind=kCustom, calls=%fused_computation | custom fusion | bytes 4194328 | tf_op jit(solution)/shard_map/while/body/eval_jaxpr/vmap(jit(dynamic_index_in_dim))/gather | solution.py:124
  242.1 1.2 fusion.51
  243.3 0.0 copy-start.5
  243.3 1.5 copy.31
  244.8 2.4 fusion.54
  247.2 0.5 copy.30
  247.8 0.0 copy-done.5
  247.8 0.3 fusion.33
  248.1 1.7 fusion.23
  249.8 0.3 copy.43
  250.1 0.2 reshape.223
  250.2 0.0 copy-start.3
  250.2 5.2 %convolution_convert_fusion = bf16[128,3584]{1,0:T(8,128)(2,1)} fusion(bf16[128,1024]{1,0:T(8,128)(2,1)S(1)} %reshape.223, bf16[1024,3584]{1,0:T(8,128)(2,1)} %param.17), kind=kOutput, calls=%fused_computation.6 | convolution fusion | flops 939982848 | bytes 8519680 | tf_op jit(solution)/shard_map/dot_general | solution.py:137
  255.4 0.0 reduce-scatter.2.cloned.1.call-update
  255.4 0.0 copy-done.3
  256.1 21.7 %reduce-scatter.2.cloned.1.call-done = bf16[32,3584]{1,0:T(8,128)(2,1)} async-done(((bf16[128,3584]{1,0:T(8,128)(2,1)}), bf16[32,3584]{1,0:T(8,128)(2,1)}) %reduce-scatter.2.cloned.1.call-update) | async-done | bytes 229392 | tf_op jit(solution)/shard_map/reduce_scatter | solution.py:136
  277.9 1.1 fusion.26
  279.0 1.8 fusion.30
  (15 shorter events, 0.2 us)
Async XLA Ops:
  6.5 57.4 %all-gather.3.cloned.1.call-start = ((), (), s32[]{:S(2)}) async-start(), calls=%async_computation.1 | async-start | bytes 9175040 | tf_op jit(solution)/shard_map/all_gather | solution.py:91
  7.3 230.8 %all-gather.5.cloned.1.call-start = ((), (), s32[]{:S(2)}) async-start(), calls=%async_computation.2 | async-start | bytes 10485760 | tf_op jit(solution)/shard_map/all_gather | solution.py:121
  64.0 5.2 %copy-start = (bf16[1024,3584]{1,0:T(8,128)(2,1)S(1)}, bf16[1024,3584]{1,0:T(8,128)(2,1)}, u32[]{:S(2)}) copy-start(bf16[1024,3584]{1,0:T(8,128)(2,1)} %all-gather.3.cloned.1.call-done) | copy-start | bytes 22020100
  86.5 1.8 copy-start.1
  88.2 189.6 %reduce-scatter.2.cloned.1.call-start = ((), (), s32[]{:S(2)}) async-start(), calls=%async_computation.3 | async-start | bytes 1146880 | tf_op jit(solution)/shard_map/reduce_scatter | solution.py:136
  105.9 3.5 %copy-start.4 = (s32[2]{0:T(128)S(1)}, s32[2]{0:T(128)}, u32[]{:S(2)}) copy-start(s32[2]{0:T(128)} %param.18) | copy-start | bytes 28
  109.5 0.7 copy-start.2
  243.3 4.5 %copy-start.5 = (f32[2,2,2,64,64]{3,4,2,1,0:T(8,128)S(1)}, f32[2,2,2,64,64]{3,4,2,1,0:T(8,128)}, u32[]{:S(2)}) copy-start(f32[2,2,2,64,64]{3,4,2,1,0:T(8,128)} %get-tuple-element.45) | copy-start | bytes 393220
  250.2 5.2 %copy-start.3 = (bf16[3584]{0:T(1024)(128)(2,1)S(1)}, bf16[3584]{0:T(1024)(128)(2,1)}, u32[]{:S(2)}) copy-start(bf16[3584]{0:T(1024)(128)(2,1)} %param.13) | copy-start | bytes 21508
Sparse Core Ops, SparseCore 0:
  8.9 55.0 all-gather.2
  88.4 149.6 all-gather.4
  255.6 22.2 reduce-scatter.1
where the time goes:
time: 288 us; the launch traced here: 287 us
  waiting for transfers between devices  203 us (70%)
  matrix products  35.3 us (12%)
  between operations  14.1 us (5%)
  other arithmetic  13.2 us (5%)
  local copies, waits for them, and re-layouts  12 us (4%)
  blocking collectives  9.35 us (3%)
    all_gather x1, waiting for transfers between devices, shards(): fetched = lax.all_gather(prepared, 'dev', axis=0, tiled=True)  127 us
    all_gather x1, waiting for transfers between devices, shards(): segment = lax.all_gather(passage_hidden, 'tp', axis=0, tiled=True)  54.1 us
    reduce_scatter x1, waiting for transfers between devices, shards(): lax.psum_scatter(settle(jnp.dot(attended, w_out, preferred_element_type=j...  21.7 us
    dot_general x2, matrix products, shards(): values = jnp.dot(normed, w_value, preferred_element_type=jnp.float32)  10.9 us
    all_gather x1, blocking collectives, shards(): segment = lax.all_gather(query_hidden, 'tp', axis=0, tiled=True)  9.35 us
    dot_general x2, matrix products, shards(): jnp.dot(normed, w_key, preferred_element_type=jnp.float32)  9.02 us
  transfers between devices with their start and end apart: 3, of which 3 were waited for; matrix products, arithmetic and copies ran while one was open for 5% of the time, Pallas kernels for 0%

commit v1 on v0

v1 whole, which is shorter than its diff:
```python
import functools

import jax
import jax.numpy as jnp
import numpy as np
from jax import lax
from jax.experimental import pallas as pl
from jax.experimental.pallas import tpu as pltpu
from jax.sharding import PartitionSpec as P

HD = 256
HALF = HD // 2
PLEN = 512
QLEN = 64
CHUNKS = 2
VMEM_LIMIT = 48 * 1024 * 1024

epsilon = 1e-06
softcap_limit = 50.0


def tables(first, count):
    frequency = (10000.0 ** (-2.0 * np.arange(HALF, dtype=np.float32) / HD)).astype(np.float32)
    positions = np.arange(first, first + count, dtype=np.float32)
    angles = (positions[:, None] * frequency[None, :]).astype(np.float32)
    return jnp.asarray(np.cos(angles)), jnp.asarray(np.sin(angles))


def normalize(rows, gain):
    values = rows.astype(jnp.float32)
    inverse_rms = lax.rsqrt(jnp.mean(values * values, axis=-1, keepdims=True) + epsilon)
    return (values * inverse_rms * gain.astype(jnp.float32)).astype(jnp.bfloat16)


def turned(raw, cosine, sine):
    low, high = raw[:, :HALF], raw[:, HALF:]
    return jnp.concatenate([low * cosine - high * sine, high * cosine + low * sine], axis=1)


def params(aliased=False):
    return pltpu.CompilerParams(vmem_limit_bytes=VMEM_LIMIT)


def passage_body(heads_kv, aliased, place, rows_ref, wk_ref, wv_ref, cos_ref, sin_ref, *rest):
    out_ref = rest[-1]
    step = pl.program_id(0)

    @pl.when(step < heads_kv)
    def _():
        raw = jnp.dot(rows_ref[...], wk_ref[...], preferred_element_type=jnp.float32)
        out_ref[...] = turned(raw, cos_ref[...], sin_ref[...]).astype(jnp.bfloat16)

    @pl.when(step >= heads_kv)
    def _():
        raw = jnp.dot(rows_ref[...], wv_ref[...], preferred_element_type=jnp.float32)
        out_ref[...] = raw.astype(jnp.bfloat16)


def passage_project(block, place, total_rows, w_key, w_value, cosine, sine, held):
    count, width = block.shape
    heads_kv = w_key.shape[1] // HD
    per_passage = PLEN // count
    in_specs = [
        pl.BlockSpec((count, width), lambda j, place: (0, 0)),
        pl.BlockSpec((width, HD), lambda j, place: (0, jnp.minimum(j, heads_kv - 1))),
        pl.BlockSpec((width, HD), lambda j, place: (0, jnp.maximum(j - heads_kv, 0))),
        pl.BlockSpec((count, HALF), lambda j, place: (lax.rem(place[0], per_passage), 0)),
        pl.BlockSpec((count, HALF), lambda j, place: (lax.rem(place[0], per_passage), 0)),
    ]
    operands = [block, w_key, w_value, cosine, sine]
    aliases = {}
    if held is not None:
        in_specs.append(pl.BlockSpec(memory_space=pl.ANY))
        operands.append(held)
        aliases = {6: 0}
    return pl.pallas_call(
        functools.partial(passage_body, heads_kv, held is not None),
        grid_spec=pltpu.PrefetchScalarGridSpec(
            num_scalar_prefetch=1,
            grid=(2 * heads_kv,),
            in_specs=in_specs,
            out_specs=pl.BlockSpec((count, HD), lambda j, place: (place[0], j)),
        ),
        out_shape=jax.ShapeDtypeStruct((total_rows, 2 * heads_kv * HD), jnp.bfloat16),
        input_output_aliases=aliases,
        compiler_params=params(),
        cost_estimate=pl.CostEstimate(
            flops=4 * count * width * heads_kv * HD,
            bytes_accessed=4 * width * heads_kv * HD + 2 * count * width,
            transcendentals=0,
        ),
    )(place.reshape(1).astype(jnp.int32), *operands)


def query_body(n_blocks, n_out, heads_q, heads_kv, order, slot, *refs):
    blocks = refs[:n_blocks]
    gain_ref, wq_ref, wk_ref, wv_ref, cos_ref, sin_ref, out_ref, normed, held = refs[n_blocks:]
    step = pl.program_id(0)
    size = blocks[0].shape[0]

    @pl.when(step == 0)
    def _():
        for i in range(n_blocks):
            start = pl.multiple_of(order[i] * size, size)
            normed[pl.ds(start, size), :] = normalize(blocks[i][...], gain_ref[...])

    def store():
        for i in range(n_out):
            start = pl.multiple_of(slot[i] * QLEN, QLEN)
            out_ref[i] = held[pl.ds(start, QLEN), :].astype(jnp.bfloat16)

    @pl.when(step < heads_q)
    def _():
        raw = jnp.dot(normed[...], wq_ref[...], preferred_element_type=jnp.float32)
        held[...] = turned(raw, cos_ref[...], sin_ref[...]) * HD ** (-0.5)
        store()

    @pl.when((step >= heads_q) & (step < heads_q + heads_kv))
    def _():
        raw = jnp.dot(normed[...], wk_ref[...], preferred_element_type=jnp.float32)
        held[...] = turned(raw, cos_ref[...], sin_ref[...])
        store()

    @pl.when(step >= heads_q + heads_kv)
    def _():
        held[...] = jnp.dot(normed[...], wv_ref[...], preferred_element_type=jnp.float32)
        store()


def query_project(blocks, order, slot, gain, w_query, w_key, w_value, pair_slots):
    size, width = blocks[0].shape
    rows = size * len(blocks)
    heads_q, heads_kv = w_query.shape[1] // HD, w_key.shape[1] // HD
    n_out = slot.shape[0]
    cosine, sine = tables(PLEN, QLEN)
    cosine, sine = jnp.tile(cosine, (pair_slots, 1)), jnp.tile(sine, (pair_slots, 1))
    fixed = lambda j, order, slot: (0, 0)
    steps = heads_q + 2 * heads_kv
    return pl.pallas_call(
        functools.partial(query_body, len(blocks), n_out, heads_q, heads_kv),
        grid_spec=pltpu.PrefetchScalarGridSpec(
            num_scalar_prefetch=2,
            grid=(steps,),
            in_specs=[pl.BlockSpec((size, width), fixed) for _ in blocks]
            + [
                pl.BlockSpec((1, width), fixed),
                pl.BlockSpec((width, HD), lambda j, o, s: (0, jnp.minimum(j, heads_q - 1))),
                pl.BlockSpec(
                    (width, HD), lambda j, o, s: (0, jnp.clip(j - heads_q, 0, heads_kv - 1))
                ),
                pl.BlockSpec(
                    (width, HD), lambda j, o, s: (0, jnp.maximum(j - heads_q - heads_kv, 0))
                ),
                pl.BlockSpec((rows, HALF), fixed),
                pl.BlockSpec((rows, HALF), fixed),
            ],
            out_specs=pl.BlockSpec((n_out, QLEN, HD), lambda j, o, s: (0, 0, j)),
            scratch_shapes=[
                pltpu.VMEM((rows, width), jnp.bfloat16),
                pltpu.VMEM((rows, HD), jnp.float32),
            ],
        ),
        out_shape=jax.ShapeDtypeStruct((n_out, QLEN, steps * HD), jnp.bfloat16),
        compiler_params=params(),
        cost_estimate=pl.CostEstimate(
            flops=2 * rows * width * steps * HD,
            bytes_accessed=2 * width * steps * HD,
            transcendentals=0,
        ),
    )(order, slot, *blocks, gain.reshape(1, width), w_query, w_key, w_value, cosine, sine)


def capped_exp(scores):
    return jnp.exp(softcap_limit * jnp.tanh(scores / softcap_limit))


def attend_body(heads_q, heads_kv, within, pair_ref, far_ref, out_ref):
    groups = heads_q // heads_kv
    over = (((1,), (1,)), ((), ()))
    rows = lax.rem(lax.broadcasted_iota(jnp.int32, (groups * QLEN, QLEN), 0), QLEN)
    causal = rows >= lax.broadcasted_iota(jnp.int32, (groups * QLEN, QLEN), 1)
    for h in range(heads_kv):
        query = jnp.concatenate(
            [pair_ref[:, (h * groups + g) * HD : (h * groups + g + 1) * HD] for g in range(groups)],
            axis=0,
        )
        key_at, value_at = (heads_q + h) * HD, (heads_q + heads_kv + h) * HD
        keys_own = pair_ref[:, key_at : key_at + HD]
        values_own = pair_ref[:, value_at : value_at + HD]
        keys_far = far_ref[:, h * HD : (h + 1) * HD]
        values_far = far_ref[:, (heads_kv + h) * HD : (heads_kv + h + 1) * HD]
        far = capped_exp(
            lax.dot_general(query, keys_far, over, preferred_element_type=jnp.float32)
        )
        near = capped_exp(
            lax.dot_general(query, keys_own, over, preferred_element_type=jnp.float32)
        )
        near = jnp.where(causal, near, 0.0)
        total = jnp.sum(far, axis=1, keepdims=True) + jnp.sum(near, axis=1, keepdims=True)
        far = (far / total).astype(jnp.bfloat16)
        near = (near / total).astype(jnp.bfloat16)
        mixed = jnp.dot(far, values_far, preferred_element_type=jnp.float32)
        mixed = mixed + jnp.dot(near, values_own, preferred_element_type=jnp.float32)
        mixed = mixed.astype(jnp.bfloat16)
        for g in range(groups):
            at = (h * groups + g) * HD
            out_ref[:, at : at + HD] = mixed[g * QLEN : (g + 1) * QLEN]


def attend(pair, far, within, heads_q, heads_kv):
    return pl.pallas_call(
        functools.partial(attend_body, heads_q, heads_kv),
        grid_spec=pltpu.PrefetchScalarGridSpec(
            num_scalar_prefetch=1,
            grid=(1,),
            in_specs=[
                pl.BlockSpec(pair.shape, lambda j, w: (0, 0)),
                pl.BlockSpec((PLEN, far.shape[1]), lambda j, w: (w[0], 0)),
            ],
            out_specs=pl.BlockSpec((QLEN, heads_q * HD), lambda j, w: (0, 0)),
        ),
        out_shape=jax.ShapeDtypeStruct((QLEN, heads_q * HD), jnp.bfloat16),
        compiler_params=params(),
        cost_estimate=pl.CostEstimate(
            flops=4 * QLEN * (PLEN + QLEN) * heads_q * HD,
            bytes_accessed=2 * PLEN * far.shape[1],
            transcendentals=2 * QLEN * (PLEN + QLEN) * heads_q,
        ),
    )(within.reshape(1).astype(jnp.int32), pair, far)


def out_body(n_in, pair_slots, n_chips, where_ref, place, *refs):
    given = refs[:n_in]
    w_ref, keep_ref, give_ref, rows, held = refs[n_in:]
    size = keep_ref.shape[0] // n_chips

    @pl.when(pl.program_id(0) == 0)
    def _():
        for s in range(pair_slots):
            for i in range(n_in):

                @pl.when(where_ref[s] == i)
                def _():
                    rows[s * QLEN : (s + 1) * QLEN, :] = given[i][...]

    held[...] = jnp.dot(rows[...], w_ref[...], preferred_element_type=jnp.float32)
    for k in range(n_chips):
        chip = lax.rem(place[0] + k, n_chips)
        mine = pl.multiple_of((chip * 2 + place[1]) * size, size)
        twin = pl.multiple_of((chip * 2 + 1 - place[1]) * size, size)
        keep_ref[k * size : (k + 1) * size, :] = held[pl.ds(mine, size), :].astype(jnp.bfloat16)
        give_ref[k * size : (k + 1) * size, :] = held[pl.ds(twin, size), :].astype(jnp.bfloat16)


def out_project(given, sources, place, w_out, pair_slots, n_chips):
    depth, width = w_out.shape
    rows = pair_slots * QLEN
    tile = 512
    half = jax.ShapeDtypeStruct((rows // 2, width), jnp.bfloat16)
    return pl.pallas_call(
        functools.partial(out_body, len(given), pair_slots, n_chips),
        grid_spec=pltpu.PrefetchScalarGridSpec(
            num_scalar_prefetch=2,
            grid=(width // tile,),
            in_specs=[pl.BlockSpec((QLEN, depth), lambda j, a, b: (0, 0)) for _ in given]
            + [pl.BlockSpec((depth, tile), lambda j, a, b: (0, j))],
            out_specs=[pl.BlockSpec((rows // 2, tile), lambda j, a, b: (0, j))] * 2,
            scratch_shapes=[
                pltpu.VMEM((rows, depth), jnp.bfloat16),
                pltpu.VMEM((rows, tile), jnp.float32),
            ],
        ),
        out_shape=[half, half],
        compiler_params=params(),
        cost_estimate=pl.CostEstimate(
            flops=2 * rows * depth * width, bytes_accessed=2 * depth * width, transcendentals=0
        ),
    )(sources, place, *given, w_out)


def shards(
    passage_hidden,
    query_hidden,
    gain_in,
    gain_out,
    w_query,
    w_key,
    w_value,
    w_out,
    pair_passage,
    pair_count,
):
    n_tp, n_dev = lax.axis_size("tp"), lax.axis_size("dev")
    n_chips = n_tp // 2
    lane, owner = lax.axis_index("tp"), lax.axis_index("dev")
    chip, core = lane // 2, lane % 2
    heads_q, heads_kv = w_query.shape[1] // HD, w_key.shape[1] // HD
    pair_slots = pair_passage.shape[0]
    block_rows = passage_hidden.shape[0]
    total_rows = block_rows * n_tp
    per_owner = total_rows // PLEN

    def to_twin(values):
        return lax.ppermute(values, "tp", [(i, i ^ 1) for i in range(n_tp)])

    def from_chip(values, k):
        return lax.ppermute(values, "tp", [((i + 2 * k) % n_tp, i) for i in range(n_tp)])

    def to_owner(values, k):
        return lax.ppermute(values, "dev", [(i, (i + k) % n_dev) for i in range(n_dev)])

    def from_owner(values, k):
        return lax.ppermute(values, "dev", [((i + k) % n_dev, i) for i in range(n_dev)])

    query_blocks, query_order = [query_hidden, to_twin(query_hidden)], [lane, lane ^ 1]
    for k in range(1, n_chips):
        far = from_chip(query_hidden, k)
        base = (chip + k) % n_chips * 2
        query_blocks += [far, to_twin(far)]
        query_order += [base + core, base + 1 - core]
    shifts = [(owner + k) % n_dev for k in range(n_dev)]
    holder = pair_passage // per_owner
    slot = jnp.zeros((n_dev,), jnp.int32)
    for s in range(1, pair_slots):
        slot = jnp.where(holder[s] == jnp.stack(shifts), s, slot)
    named = [pair_passage] + [to_owner(pair_passage, k) for k in range(1, n_dev)]
    within = []
    for pairs in named:
        pick = pairs[0]
        for s in range(1, pair_slots):
            pick = jnp.where(pairs[s] // per_owner == owner, pairs[s], pick)
        within.append(pick % per_owner)

    normed = normalize(passage_hidden, gain_in)
    twin = to_twin(normed)
    unit = block_rows // CHUNKS
    arrivals = []
    for k in range(1, n_chips):
        for c in range(CHUNKS):
            far = from_chip(normed[c * unit : (c + 1) * unit], k)
            arrivals.append((k, c, far, to_twin(far)))

    projected = query_project(
        query_blocks,
        jnp.stack(query_order).astype(jnp.int32),
        slot,
        gain_in,
        w_query,
        w_key,
        w_value,
        pair_slots,
    )
    pairs = [projected[0]] + [to_owner(projected[k], k) for k in range(1, n_dev)]

    cosine, sine = tables(0, PLEN)
    project = functools.partial(
        passage_project, total_rows=total_rows, w_key=w_key, w_value=w_value, cosine=cosine, sine=sine
    )
    held = project(normed, lane, held=None)
    held = project(twin, lane ^ 1, held=held)
    for k, c, mine, other in arrivals:
        base = (chip + k) % n_chips * 2
        held = project(mine, (base + core) * CHUNKS + c, held=held)
        held = project(other, (base + 1 - core) * CHUNKS + c, held=held)

    mixed = [None] * n_dev
    for k in list(range(1, n_dev)) + [0]:
        result = attend(pairs[k], held, within[k], heads_q, heads_kv)
        mixed[k] = result if k == 0 else from_owner(result, k)

    sources = (holder - owner + n_dev) % n_dev
    keep, give = out_project(
        mixed,
        sources.astype(jnp.int32),
        jnp.stack([chip, core]).astype(jnp.int32),
        w_out,
        pair_slots,
        n_chips,
    )
    size = query_hidden.shape[0]
    summed = keep.astype(jnp.float32) + to_twin(give).astype(jnp.float32)
    merged = summed[:size]
    for k in range(1, n_chips):
        sent = summed[k * size : (k + 1) * size].astype(jnp.bfloat16)
        merged = merged + from_chip(sent, n_chips - k).astype(jnp.float32)
    inverse_rms = lax.rsqrt(jnp.mean(merged * merged, axis=-1, keepdims=True) + epsilon)
    branch = merged * inverse_rms * gain_out.astype(jnp.float32)
    row_ids = lane * size + jnp.arange(size)
    alive = row_ids // QLEN < pair_count[0]
    layer_out = jnp.where(alive[:, None], query_hidden.astype(jnp.float32) + branch, 0.0)
    return layer_out.astype(jnp.bfloat16)


def solution(mesh):
    placed = (
        P(("grp", "dev", "tp"), None),
        P(("grp", "dev", "tp"), None),
        P(),
        P(),
        P(None, "tp"),
        P(None, "tp"),
        P(None, "tp"),
        P("tp", None),
        P(("grp", "dev")),
        P(("grp", "dev")),
    )
    return jax.shard_map(
        shards, mesh=mesh, in_specs=placed, out_specs=P(("grp", "dev", "tp"), None), check_vma=False
    )
```

time: 288 us -> 145 us (0.50)
  waiting for transfers between devices: 203 us -> 40.3 us
  Pallas kernels: 0 us -> 53.3 us
  matrix products: 35.3 us -> 0 us
  starting transfers between devices: 0.08 us -> 21.1 us
  blocking collectives: 9.35 us -> 0 us
  other arithmetic: 13.2 us -> 6.49 us
  local copies, waits for them, and re-layouts: 12 us -> 7.9 us
    all_gather x2 -> x0, waiting for transfers between devices: 181 us -> none  [the longest x1 127 us: shards(): fetched = lax.all_gather(prepared, 'dev', axis=0, tiled=True)]
    pallas_call x0 -> x12, Pallas kernels: none -> 53.3 us  [the longest x6 33.1 us: passage_project(): pl.pallas_call(functools.partial(passage_body, heads_kv, held is not None...]
    ppermute x0 -> x19, waiting for transfers between devices: none -> 40.3 us  [the longest x4 28 us: from_chip(): lax.ppermute(values, 'tp', [((i + 2 * k) % n_tp, i) for i in range(n_tp)])]
    dot_general x10 -> x0, matrix products: 35.3 us -> none  [the longest x2 10.9 us: shards(): values = jnp.dot(normed, w_value, preferred_element_type=jnp.float32)]
    reduce_scatter x1 -> x0, waiting for transfers between devices: 21.7 us -> none  [shards(): lax.psum_scatter(settle(jnp.dot(attended, w_out, preferred_element_type=j...]
    ppermute x0 -> x19, starting transfers between devices: none -> 21.1 us  [the longest x6 9.08 us: to_owner(): lax.ppermute(values, 'dev', [(i, (i + k) % n_dev) for i in range(n_dev)])]
    all_gather x1 -> x0, blocking collectives: 9.35 us -> none  [shards(): segment = lax.all_gather(query_hidden, 'tp', axis=0, tiled=True)]
    gather x1 -> x0, local copies, waits for them, and re-layouts: 4.06 us -> none  [one_pair(): lax.dynamic_index_in_dim(fetched, passage_row, 0, keepdims=False)]
  transfers between devices with their start and end apart: 3 -> 19, of which waited for: 3 -> 7; matrix products, arithmetic and copies ran while one was open for 5% -> 5% of each run, Pallas kernels for 0% -> 32%
where the time goes in v1:
time: 145 us; the launch traced here: 144 us
  Pallas kernels  53.3 us (37%)
  waiting for transfers between devices  40.3 us (28%)
  starting transfers between devices  21.1 us (15%)
  between operations  15 us (10%)
  local copies, waits for them, and re-layouts  7.9 us (5%)
  other arithmetic  6.49 us (4%)
    pallas_call x6, Pallas kernels, passage_project(): pl.pallas_call(functools.partial(passage_body, heads_kv, held is not None...  33.1 us
    ppermute x4, waiting for transfers between devices, from_chip(): lax.ppermute(values, 'tp', [((i + 2 * k) % n_tp, i) for i in range(n_tp)])  28 us
    ppermute x6, waiting for transfers between devices, to_owner(): lax.ppermute(values, 'dev', [(i, (i + k) % n_dev) for i in range(n_dev)])  9.77 us
    pallas_call x1, Pallas kernels, query_project(): pl.pallas_call(functools.partial(query_body, len(blocks), n_out, heads_q,...  9.43 us
    ppermute x6, starting transfers between devices, to_owner(): lax.ppermute(values, 'dev', [(i, (i + k) % n_dev) for i in range(n_dev)])  9.08 us
    pallas_call x1, Pallas kernels, out_project(): pl.pallas_call(functools.partial(out_body, len(given), pair_slots, n_chip...  6.93 us
    ppermute x4, starting transfers between devices, from_chip(): lax.ppermute(values, 'tp', [((i + 2 * k) % n_tp, i) for i in range(n_tp)])  5.72 us
    ppermute x3, starting transfers between devices, from_owner(): lax.ppermute(values, 'dev', [((i + k) % n_dev, i) for i in range(n_dev)])  5.03 us
  transfers between devices with their start and end apart: 19, of which 7 were waited for; matrix products, arithmetic and copies ran while one was open for 5% of the time, Pallas kernels for 32%

profile of v1, /device:TPU:0, one launch (start us, length us, event | category | flops | bytes accessed | tf_op | source)
XLA Modules:
  0.0 144.1 jit_solution(17162011234994894209)
XLA Ops:
  0.0 0.8 convert_element_type.30
  0.8 1.9 %fusion = f32[256]{0:T(256)S(1)} fusion(bf16[256,3584]{1,0:T(8,128)(2,1)} %param.14), kind=kLoop, calls=%fused_computation.2 | loop fusion | flops 2752256 | bytes 1836032 | tf_op jit(solution)/shard_map/reduce_sum | solution.py:31
  2.8 1.8 %fusion.2.rows_ref = bf16[256,3584]{1,0:T(8,128)(2,1)} fusion(bf16[256,3584]{1,0:T(8,128)(2,1)S(1)} %copy-done.4, f32[3584]{0:T(1024)S(1)} %convert_element_type.30, f32[256]{0:T(256)S(1)} %add_rsqrt_fusion), kind=kLoop, calls=%fused_computation.4 | loop fusion | flops 3670016 | bytes 3685376 | tf_op jit(solution)/shard_map/convert_element_type | solution.py:32
  4.6 0.0 copy-start.2
  4.6 0.5 collective-permute-start.7
  5.1 2.8 %fusion.5 = (bf16[128,3584]{1,0:T(8,128)(2,1)}, bf16[128,3584]{1,0:T(8,128)(2,1)}) fusion(bf16[256,3584]{1,0:T(8,128)(2,1)} %fusion.2.rows_ref), kind=kLoop, calls=%fused_computation.32 | loop fusion | bytes 3670016 | tf_op jit(solution)/shard_map/slice | solution.py:340
  7.9 2.7 %collective-permute-start.5 = (bf16[128,3584]{1,0:T(8,128)(2,1)}, bf16[128,3584]{1,0:T(8,128)(2,1)}, u32[]{:S(2)}, u32[]{:S(2)}) collective-permute-start(bf16[128,3584]{1,0:T(8,128)(2,1)} %get-tuple-element.11), channel_id=1, source_target_pairs={{2,0},{3,1},{0,2},{1,3},{6,4},{7,5},{4,6},{5,7},{10,8},{11,9},{8,1... | collective-permute-start | bytes 2752520 | tf_op jit(solution)/shard_map/ppermute | solution.py:307
  10.6 0.0 collective-permute-start.3
  10.6 4.1 %collective-permute-start.14 = (s32[2]{0:T(128)S(1)}, s32[2]{0:T(128)S(1)}, u32[]{:S(2)}, u32[]{:S(2)}) collective-permute-start(s32[2]{0:T(128)S(1)} %copy-done.9), channel_id=1, source_target_pairs={{0,12},{4,0},{8,4},{12,8},{1,13},{5,1},{9,5},{13,9},{2,14},{6,2},{... | collective-permute-start | bytes 32 | tf_op jit(solution)/shard_map/ppermute | solution.py:310
  14.7 1.5 %collective-permute-start.1 = (bf16[32,3584]{1,0:T(8,128)(2,1)S(1)}, bf16[32,3584]{1,0:T(8,128)(2,1)S(1)}, u32[]{:S(2)}, u32[]{:S(2)}) collective-permute-start(bf16[32,3584]{1,0:T(8,128)(2,1)S(1)} %copy-done.3), channel_id=1, source_target_pairs={{2,0},{3,1},{0,2},{1,3},{6,4},{7,5},{4,6},{5,7},{10,8},{11,9},{8,1... | collective-permute-start | bytes 688136 | tf_op jit(solution)/shard_map/ppermute | solution.py:307
  16.3 0.6 slice.58
  16.9 0.6 compare_select_fusion.2
  17.6 0.0 copy-start.6
  17.6 0.0 copy-start.5
  17.6 6.2 %shard_map.137.rest_0_ = bf16[1024,1024]{1,0:T(8,128)(2,1)S(1)} custom-call(s32[1]{0:T(128)} %bitcast.6.place, bf16[256,3584]{1,0:T(8,128)(2,1)} %fusion.2.rows_ref, bf16[3584,512]{1,0:T(8,128)(2,1)} %wk_ref.11, bf16[3584,512]{1,0:T(8,128)(2,1)} %wv_ref.11, f32[512,128]{1,0:T(8,128)S(1)} %copy-done.1, f32[512,128]{1,0:T(8,128)S(1)} %copy-done.2), custom_call_target="tpu_custom_call" | custom-call | flops 1879048192 | bytes 9175040 | tf_op jit(solution)/shard_map/pallas_call | solution.py:76
  23.8 0.1 collective-permute-start.11
  23.9 4.4 %collective-permute-done.11 = s32[2]{0:T(128)S(1)} collective-permute-done((s32[2]{0:T(128)S(1)}, s32[2]{0:T(128)S(1)}, u32[]{:S(2)}, u32[]{:S(2)}) %collective-permute-start.11) | collective-permute-done | bytes 40 | tf_op jit(solution)/shard_map/ppermute | solution.py:310
  28.3 0.0 collective-permute-start.8
  28.3 5.3 %collective-permute-done.8 = s32[2]{0:T(128)S(1)} collective-permute-done((s32[2]{0:T(128)S(1)}, s32[2]{0:T(128)S(1)}, u32[]{:S(2)}, u32[]{:S(2)}) %collective-permute-start.8) | collective-permute-done | bytes 40 | tf_op jit(solution)/shard_map/ppermute | solution.py:310
  33.7 22.6 %collective-permute-done.1.refs_2_ = bf16[32,3584]{1,0:T(8,128)(2,1)S(1)} collective-permute-done((bf16[32,3584]{1,0:T(8,128)(2,1)S(1)}, bf16[32,3584]{1,0:T(8,128)(2,1)S(1)}, u32[]{:S(2)}, u32[]{:S(2)}) %collective-permute-start.1) | collective-permute-done | bytes 229408 | tf_op jit(solution)/shard_map/ppermute | solution.py:307
  56.2 0.0 collective-permute-start.2
  56.2 0.6 fusion.6
  60.2 0.6 fusion.7
  64.1 0.6 fusion.8
  68.1 0.0 collective-permute-done.5.rows_ref
  68.1 0.6 collective-permute-start.6
  68.7 0.0 copy-start
  68.7 2.0 %copy-done = bf16[3584,512]{1,0:T(8,128)(2,1)S(1)} copy-done((bf16[3584,512]{1,0:T(8,128)(2,1)S(1)}, bf16[3584,512]{1,0:T(8,128)(2,1)}, u32[]{:S(2)}) %copy-start) | copy-done | bytes 3670040
  70.8 9.4 %shard_map.136 = bf16[4,64,2048]{2,1,0:T(8,128)(2,1)S(1)} custom-call(s32[4]{0:T(128)S(1)} %get-tuple-element.26.order, s32[4]{0:T(128)S(1)} %get-tuple-element.25.slot, bf16[32,3584]{1,0:T(8,128)(2,1)S(1)} %copy-done.3, bf16[32,3584]{1,0:T(8,128)(2,1)S(1)} %collective-permute-done.refs_1_, bf16[32,3584]{1,0:T(8,128)(2,1)S(1)} %collective-permute-done.1.refs_2_, ...), custom_call_target="tpu_custom_call" | custom-call | flops 1879048192 | bytes 14680064 | tf_op jit(solution)/shard_map/pallas_call | solution.py:139
  80.2 0.1 collective-permute-start.4
  80.3 0.1 slice_bitcast_fusion
  80.4 3.9 %collective-permute-start.15 = (bf16[64,2048]{1,0:T(8,128)(2,1)S(1)}, bf16[64,2048]{1,0:T(8,128)(2,1)S(1)}, u32[]{:S(2)}, u32[]{:S(2)}) collective-permute-start(bf16[64,2048]{1,0:T(8,128)(2,1)S(1)} %get-tuple-element.13), channel_id=1, source_target_pairs={{0,12},{4,0},{8,4},{12,8},{1,13},{5,1},{9,5},{13,9},{2,14},{6,2},{... | collective-permute-start | bytes 786440 | tf_op jit(solution)/shard_map/ppermute | solution.py:310
  84.3 0.0 collective-permute-start.12
  84.3 0.0 collective-permute-done.7.rows_ref
  84.3 1.0 collective-permute-start.9
  85.3 6.2 %shard_map.138.rest_0_ = bf16[1024,1024]{1,0:T(8,128)(2,1)S(1)} custom-call(s32[1]{0:T(128)} %bitcast.7.place, bf16[256,3584]{1,0:T(8,128)(2,1)} %collective-permute-done.7.rows_ref, bf16[3584,512]{1,0:T(8,128)(2,1)} %wk_ref.11, bf16[3584,512]{1,0:T(8,128)(2,1)} %wv_ref.11, f32[512,128]{1,0:T(8,128)S(1)} %copy-done.1, ...), custom_call_target="tpu_custom_call", output_to_operand_aliasing={{}: (6, {})} | custom-call | flops 1879048192 | bytes 9175040 | tf_op jit(solution)/shard_map/pallas_call | solution.py:76
  91.5 5.3 %shard_map.139.rest_0_ = bf16[1024,1024]{1,0:T(8,128)(2,1)S(1)} custom-call(s32[1]{0:T(128)} %bitcast.21.place, bf16[128,3584]{1,0:T(8,128)(2,1)} %collective-permute-done.5.rows_ref, bf16[3584,512]{1,0:T(8,128)(2,1)} %wk_ref.11, bf16[3584,512]{1,0:T(8,128)(2,1)} %wv_ref.11, f32[512,128]{1,0:T(8,128)S(1)} %copy-done.1, ...), custom_call_target="tpu_custom_call", output_to_operand_aliasing={{}: (6, {})} | custom-call | flops 939524096 | bytes 8257536 | tf_op jit(solution)/shard_map/pallas_call | solution.py:76
  96.8 0.0 collective-permute-done.6.rows_ref
  96.8 5.0 %shard_map.140.rest_0_ = bf16[1024,1024]{1,0:T(8,128)(2,1)S(1)} custom-call(s32[1]{0:T(128)} %bitcast.20.place, bf16[128,3584]{1,0:T(8,128)(2,1)S(1)} %collective-permute-done.6.rows_ref, bf16[3584,512]{1,0:T(8,128)(2,1)} %wk_ref.11, bf16[3584,512]{1,0:T(8,128)(2,1)} %wv_ref.11, f32[512,128]{1,0:T(8,128)S(1)} %copy-done.1, ...), custom_call_target="tpu_custom_call", output_to_operand_aliasing={{}: (6, {})} | custom-call | flops 939524096 | bytes 8257536 | tf_op jit(solution)/shard_map/pallas_call | solution.py:76
  101.9 5.3 %shard_map.141.rest_0_ = bf16[1024,1024]{1,0:T(8,128)(2,1)S(1)} custom-call(s32[1]{0:T(128)} %bitcast.19.place, bf16[128,3584]{1,0:T(8,128)(2,1)} %collective-permute-done.3.rows_ref, bf16[3584,512]{1,0:T(8,128)(2,1)} %wk_ref.11, bf16[3584,512]{1,0:T(8,128)(2,1)} %wv_ref.11, f32[512,128]{1,0:T(8,128)S(1)} %copy-done.1, ...), custom_call_target="tpu_custom_call", output_to_operand_aliasing={{}: (6, {})} | custom-call | flops 939524096 | bytes 8257536 | tf_op jit(solution)/shard_map/pallas_call | solution.py:76
  107.2 5.0 %shard_map.142.far_ref = bf16[1024,1024]{1,0:T(8,128)(2,1)S(1)} custom-call(s32[1]{0:T(128)} %bitcast.18.place, bf16[128,3584]{1,0:T(8,128)(2,1)S(1)} %collective-permute-done.4.rows_ref, bf16[3584,512]{1,0:T(8,128)(2,1)} %wk_ref.11, bf16[3584,512]{1,0:T(8,128)(2,1)} %wv_ref.11, f32[512,128]{1,0:T(8,128)S(1)} %copy-done.1, ...), custom_call_target="tpu_custom_call", output_to_operand_aliasing={{}: (6, {})} | custom-call | flops 939524096 | bytes 8257536 | tf_op jit(solution)/shard_map/pallas_call | solution.py:76
  112.3 0.0 collective-permute-done.15.pair_ref
  112.3 1.0 shard_map.146
  113.2 2.5 %collective-permute-start.16 = (bf16[64,1024]{1,0:T(8,128)(2,1)S(1)}, bf16[64,1024]{1,0:T(8,128)(2,1)S(1)}, u32[]{:S(2)}, u32[]{:S(2)}) collective-permute-start(bf16[64,1024]{1,0:T(8,128)(2,1)S(1)} %shard_map.146), channel_id=1, source_target_pairs={{12,0},{0,4},{4,8},{8,12},{13,1},{1,5},{5,9},{9,13},{14,2},{2,6},{... | collective-permute-start | bytes 393224 | tf_op jit(solution)/shard_map/ppermute | solution.py:313
  115.8 0.0 collective-permute-done.12.pair_ref
  115.8 1.0 shard_map.145
  116.7 1.0 collective-permute-start.13
  117.7 0.0 collective-permute-done.9.pair_ref
  117.7 1.0 shard_map.144
  118.7 1.5 %collective-permute-start.10 = (bf16[64,1024]{1,0:T(8,128)(2,1)S(1)}, bf16[64,1024]{1,0:T(8,128)(2,1)S(1)}, u32[]{:S(2)}, u32[]{:S(2)}) collective-permute-start(bf16[64,1024]{1,0:T(8,128)(2,1)S(1)} %shard_map.144), channel_id=1, source_target_pairs={{4,0},{8,4},{12,8},{0,12},{5,1},{9,5},{13,9},{1,13},{6,2},{10,6},{... | collective-permute-start | bytes 393224 | tf_op jit(solution)/shard_map/ppermute | solution.py:313
  120.2 0.6 fusion.9
  124.6 0.1 pad_add_fusion.place
  124.7 0.9 shard_map.143.refs_0_
  125.7 0.2 collective-permute-done.13.refs_2_
  125.9 0.5 collective-permute-done.10.refs_1_
  126.4 6.9 %shard_map.147 = (bf16[64,3584]{1,0:T(8,128)(2,1)S(1)}, bf16[64,3584]{1,0:T(8,128)(2,1)S(1)}) custom-call(s32[2]{0:T(128)S(1)} %get-tuple-element.9.where_ref, s32[2]{0:T(128)S(1)} %pad_add_fusion.place, bf16[64,1024]{1,0:T(8,128)(2,1)S(1)} %shard_map.143.refs_0_, bf16[64,1024]{1,0:T(8,128)(2,1)S(1)} %collective-permute-done.10.refs_1_, ...), custom_call_target="tpu_custom_call" | custom-call | flops 939524096 | bytes 7340032 | tf_op jit(solution)/shard_map/pallas_call | solution.py:260
  133.3 0.0 copy-start.8
  133.3 0.1 collective-permute-start.17
  133.4 1.8 %collective-permute-done.17 = bf16[64,3584]{1,0:T(8,128)(2,1)S(1)} collective-permute-done((bf16[64,3584]{1,0:T(8,128)(2,1)S(1)}, bf16[64,3584]{1,0:T(8,128)(2,1)S(1)}, u32[]{:S(2)}, u32[]{:S(2)}) %collective-permute-start.17) | collective-permute-done | bytes 458784 | tf_op jit(solution)/shard_map/ppermute | solution.py:304
  135.2 0.1 convert_add_fusion
  135.4 1.6 %collective-permute-start.18 = (bf16[32,3584]{1,0:T(8,128)(2,1)S(1)}, bf16[32,3584]{1,0:T(8,128)(2,1)S(1)}, u32[]{:S(2)}, u32[]{:S(2)}) collective-permute-start(bf16[32,3584]{1,0:T(8,128)(2,1)S(1)} %slice.91), channel_id=1, source_target_pairs={{2,0},{3,1},{0,2},{1,3},{6,4},{7,5},{4,6},{5,7},{10,8},{11,9},{8,1... | collective-permute-start | bytes 688136 | tf_op jit(solution)/shard_map/ppermute | solution.py:307
  137.6 5.5 %collective-permute-done.18 = bf16[32,3584]{1,0:T(8,128)(2,1)S(1)} collective-permute-done((bf16[32,3584]{1,0:T(8,128)(2,1)S(1)}, bf16[32,3584]{1,0:T(8,128)(2,1)S(1)}, u32[]{:S(2)}, u32[]{:S(2)}) %collective-permute-start.18) | collective-permute-done | bytes 229408 | tf_op jit(solution)/shard_map/ppermute | solution.py:307
  143.1 0.2 multiply_reduce_fusion
  143.3 0.8 select_convert_fusion
  (30 shorter events, 0.1 us)
Async XLA Ops:
  0.0 2.8 %copy-start.4 = (bf16[256,3584]{1,0:T(8,128)(2,1)S(1)}, bf16[256,3584]{1,0:T(8,128)(2,1)}, u32[]{:S(2)}) copy-start(bf16[256,3584]{1,0:T(8,128)(2,1)} %param.14) | copy-start | bytes 5505028
  4.6 6.0 %copy-start.9 = (s32[2]{0:T(128)S(1)}, s32[2]{0:T(128)}, u32[]{:S(2)}) copy-start(s32[2]{0:T(128)} %param.22) | copy-start | bytes 28
  4.6 10.1 %copy-start.3 = (bf16[32,3584]{1,0:T(8,128)(2,1)S(1)}, bf16[32,3584]{1,0:T(8,128)(2,1)}, u32[]{:S(2)}) copy-start(bf16[32,3584]{1,0:T(8,128)(2,1)} %refs_0_.1) | copy-start | bytes 688132
  4.6 12.9 %copy-start.7 = (bf16[3584]{0:T(1024)(128)(2,1)S(1)}, bf16[3584]{0:T(1024)(128)(2,1)}, u32[]{:S(2)}) copy-start(bf16[3584]{0:T(1024)(128)(2,1)} %param.16) | copy-start | bytes 21508
  4.6 13.0 %copy-start.1 = (f32[512,128]{1,0:T(8,128)S(1)}, f32[512,128]{1,0:T(8,128)}, u32[]{:S(2)}) copy-start(f32[512,128]{1,0:T(8,128)} %constant.161.clone.cos_ref) | copy-start | bytes 786436
  4.6 13.0 %copy-start.2 = (f32[512,128]{1,0:T(8,128)S(1)}, f32[512,128]{1,0:T(8,128)}, u32[]{:S(2)}) copy-start(f32[512,128]{1,0:T(8,128)} %constant.162.clone.sin_ref) | copy-start | bytes 786436
  4.6 79.7 %collective-permute-start.7 = (bf16[256,3584]{1,0:T(8,128)(2,1)}, bf16[256,3584]{1,0:T(8,128)(2,1)}, u32[]{:S(2)}, u32[]{:S(2)}) collective-permute-start(bf16[256,3584]{1,0:T(8,128)(2,1)} %fusion.2.rows_ref), channel_id=1, source_target_pairs={{0,1},{1,0},{2,3},{3,2},{4,5},{5,4},{6,7},{7,6},{8,9},{9,8},{10,11... | collective-permute-start | bytes 5505032 | tf_op jit(solution)/shard_map/ppermute | solution.py:304
  7.9 60.2 %collective-permute-start.5 = (bf16[128,3584]{1,0:T(8,128)(2,1)}, bf16[128,3584]{1,0:T(8,128)(2,1)}, u32[]{:S(2)}, u32[]{:S(2)}) collective-permute-start(bf16[128,3584]{1,0:T(8,128)(2,1)} %get-tuple-element.11), channel_id=1, source_target_pairs={{2,0},{3,1},{0,2},{1,3},{6,4},{7,5},{4,6},{5,7},{10,8},{11,9},{8,1... | collective-permute-start | bytes 2752520 | tf_op jit(solution)/shard_map/ppermute | solution.py:307
  10.6 69.6 %collective-permute-start.3 = (bf16[128,3584]{1,0:T(8,128)(2,1)}, bf16[128,3584]{1,0:T(8,128)(2,1)}, u32[]{:S(2)}, u32[]{:S(2)}) collective-permute-start(bf16[128,3584]{1,0:T(8,128)(2,1)} %get-tuple-element.12), channel_id=1, source_target_pairs={{2,0},{3,1},{0,2},{1,3},{6,4},{7,5},{4,6},{5,7},{10,8},{11,9},{8,1... | collective-permute-start | bytes 2752520 | tf_op jit(solution)/shard_map/ppermute | solution.py:307
  10.6 13.2 %collective-permute-start.14 = (s32[2]{0:T(128)S(1)}, s32[2]{0:T(128)S(1)}, u32[]{:S(2)}, u32[]{:S(2)}) collective-permute-start(s32[2]{0:T(128)S(1)} %copy-done.9), channel_id=1, source_target_pairs={{0,12},{4,0},{8,4},{12,8},{1,13},{5,1},{9,5},{13,9},{2,14},{6,2},{... | collective-permute-start | bytes 32 | tf_op jit(solution)/shard_map/ppermute | solution.py:310
  14.7 41.5 %collective-permute-start.1 = (bf16[32,3584]{1,0:T(8,128)(2,1)S(1)}, bf16[32,3584]{1,0:T(8,128)(2,1)S(1)}, u32[]{:S(2)}, u32[]{:S(2)}) collective-permute-start(bf16[32,3584]{1,0:T(8,128)(2,1)S(1)} %copy-done.3), channel_id=1, source_target_pairs={{2,0},{3,1},{0,2},{1,3},{6,4},{7,5},{4,6},{5,7},{10,8},{11,9},{8,1... | collective-permute-start | bytes 688136 | tf_op jit(solution)/shard_map/ppermute | solution.py:307
  17.6 51.1 %copy-start.6 = (f32[64,128]{1,0:T(8,128)S(1)}, f32[64,128]{1,0:T(8,128)}, u32[]{:S(2)}) copy-start(f32[64,128]{1,0:T(8,128)} %constant.159.clone) | copy-start | bytes 98308
  17.6 51.1 %copy-start.5 = (f32[64,128]{1,0:T(8,128)S(1)}, f32[64,128]{1,0:T(8,128)}, u32[]{:S(2)}) copy-start(f32[64,128]{1,0:T(8,128)} %constant.160.clone) | copy-start | bytes 98308
  23.8 4.5 %collective-permute-start.11 = (s32[2]{0:T(128)S(1)}, s32[2]{0:T(128)S(1)}, u32[]{:S(2)}, u32[]{:S(2)}) collective-permute-start(s32[2]{0:T(128)S(1)} %copy-done.9), channel_id=1, source_target_pairs={{0,8},{4,12},{8,0},{12,4},{1,9},{5,13},{9,1},{13,5},{2,10},{6,14},... | collective-permute-start | bytes 32 | tf_op jit(solution)/shard_map/ppermute | solution.py:310
  28.3 5.3 %collective-permute-start.8 = (s32[2]{0:T(128)S(1)}, s32[2]{0:T(128)S(1)}, u32[]{:S(2)}, u32[]{:S(2)}) collective-permute-start(s32[2]{0:T(128)S(1)} %copy-done.9), channel_id=1, source_target_pairs={{0,4},{4,8},{8,12},{12,0},{1,5},{5,9},{9,13},{13,1},{2,6},{6,10},{... | collective-permute-start | bytes 32 | tf_op jit(solution)/shard_map/ppermute | solution.py:310
  33.7 35.0 %collective-permute-start = (bf16[32,3584]{1,0:T(8,128)(2,1)S(1)}, bf16[32,3584]{1,0:T(8,128)(2,1)S(1)}, u32[]{:S(2)}, u32[]{:S(2)}) collective-permute-start(bf16[32,3584]{1,0:T(8,128)(2,1)S(1)} %copy-done.3), channel_id=1, source_target_pairs={{0,1},{1,0},{2,3},{3,2},{4,5},{5,4},{6,7},{7,6},{8,9},{9,8},{10,11... | collective-permute-start | bytes 688136 | tf_op jit(solution)/shard_map/ppermute | solution.py:304
  56.2 12.4 %collective-permute-start.2 = (bf16[32,3584]{1,0:T(8,128)(2,1)S(1)}, bf16[32,3584]{1,0:T(8,128)(2,1)}, u32[]{:S(2)}, u32[]{:S(2)}) collective-permute-start(bf16[32,3584]{1,0:T(8,128)(2,1)S(1)} %collective-permute-done.1.refs_2_), channel_id=1, source_target_pairs={{0,1},{1,0},{2,3},{3,2},{4,5},{5,4},{6,7},{7,6},{8,9},{9,8},{10,11... | collective-permute-start | bytes 688136 | tf_op jit(solution)/shard_map/ppermute | solution.py:304
  68.1 28.7 %collective-permute-start.6 = (bf16[128,3584]{1,0:T(8,128)(2,1)}, bf16[128,3584]{1,0:T(8,128)(2,1)S(1)}, u32[]{:S(2)}, u32[]{:S(2)}) collective-permute-start(bf16[128,3584]{1,0:T(8,128)(2,1)} %collective-permute-done.5.rows_ref), channel_id=1, source_target_pairs={{0,1},{1,0},{2,3},{3,2},{4,5},{5,4},{6,7},{7,6},{8,9},{9,8},{10,11... | collective-permute-start | bytes 2752520 | tf_op jit(solution)/shard_map/ppermute | solution.py:304
  68.7 2.0 %copy-start = (bf16[3584,512]{1,0:T(8,128)(2,1)S(1)}, bf16[3584,512]{1,0:T(8,128)(2,1)}, u32[]{:S(2)}) copy-start(bf16[3584,512]{1,0:T(8,128)(2,1)} %wk_ref.11) | copy-start | bytes 11010052
  80.2 27.0 %collective-permute-start.4 = (bf16[128,3584]{1,0:T(8,128)(2,1)}, bf16[128,3584]{1,0:T(8,128)(2,1)S(1)}, u32[]{:S(2)}, u32[]{:S(2)}) collective-permute-start(bf16[128,3584]{1,0:T(8,128)(2,1)} %collective-permute-done.3.rows_ref), channel_id=1, source_target_pairs={{0,1},{1,0},{2,3},{3,2},{4,5},{5,4},{6,7},{7,6},{8,9},{9,8},{10,11... | collective-permute-start | bytes 2752520 | tf_op jit(solution)/shard_map/ppermute | solution.py:304
  80.4 31.9 %collective-permute-start.15 = (bf16[64,2048]{1,0:T(8,128)(2,1)S(1)}, bf16[64,2048]{1,0:T(8,128)(2,1)S(1)}, u32[]{:S(2)}, u32[]{:S(2)}) collective-permute-start(bf16[64,2048]{1,0:T(8,128)(2,1)S(1)} %get-tuple-element.13), channel_id=1, source_target_pairs={{0,12},{4,0},{8,4},{12,8},{1,13},{5,1},{9,5},{13,9},{2,14},{6,2},{... | collective-permute-start | bytes 786440 | tf_op jit(solution)/shard_map/ppermute | solution.py:310
  84.3 31.5 %collective-permute-start.12 = (bf16[64,2048]{1,0:T(8,128)(2,1)S(1)}, bf16[64,2048]{1,0:T(8,128)(2,1)S(1)}, u32[]{:S(2)}, u32[]{:S(2)}) collective-permute-start(bf16[64,2048]{1,0:T(8,128)(2,1)S(1)} %get-tuple-element.14), channel_id=1, source_target_pairs={{0,8},{4,12},{8,0},{12,4},{1,9},{5,13},{9,1},{13,5},{2,10},{6,14},... | collective-permute-start | bytes 786440 | tf_op jit(solution)/shard_map/ppermute | solution.py:310
  84.3 33.4 %collective-permute-start.9 = (bf16[64,2048]{1,0:T(8,128)(2,1)S(1)}, bf16[64,2048]{1,0:T(8,128)(2,1)S(1)}, u32[]{:S(2)}, u32[]{:S(2)}) collective-permute-start(bf16[64,2048]{1,0:T(8,128)(2,1)S(1)} %get-tuple-element.15), channel_id=1, source_target_pairs={{0,4},{4,8},{8,12},{12,0},{1,5},{5,9},{9,13},{13,1},{2,6},{6,10},{... | collective-permute-start | bytes 786440 | tf_op jit(solution)/shard_map/ppermute | solution.py:310
  113.2 12.4 %collective-permute-start.16 = (bf16[64,1024]{1,0:T(8,128)(2,1)S(1)}, bf16[64,1024]{1,0:T(8,128)(2,1)S(1)}, u32[]{:S(2)}, u32[]{:S(2)}) collective-permute-start(bf16[64,1024]{1,0:T(8,128)(2,1)S(1)} %shard_map.146), channel_id=1, source_target_pairs={{12,0},{0,4},{4,8},{8,12},{13,1},{1,5},{5,9},{9,13},{14,2},{2,6},{... | collective-permute-start | bytes 393224 | tf_op jit(solution)/shard_map/ppermute | solution.py:313
  116.7 9.2 %collective-permute-start.13 = (bf16[64,1024]{1,0:T(8,128)(2,1)S(1)}, bf16[64,1024]{1,0:T(8,128)(2,1)S(1)}, u32[]{:S(2)}, u32[]{:S(2)}) collective-permute-start(bf16[64,1024]{1,0:T(8,128)(2,1)S(1)} %shard_map.145), channel_id=1, source_target_pairs={{8,0},{12,4},{0,8},{4,12},{9,1},{13,5},{1,9},{5,13},{10,2},{14,6},... | collective-permute-start | bytes 393224 | tf_op jit(solution)/shard_map/ppermute | solution.py:313
  118.7 7.7 %collective-permute-start.10 = (bf16[64,1024]{1,0:T(8,128)(2,1)S(1)}, bf16[64,1024]{1,0:T(8,128)(2,1)S(1)}, u32[]{:S(2)}, u32[]{:S(2)}) collective-permute-start(bf16[64,1024]{1,0:T(8,128)(2,1)S(1)} %shard_map.144), channel_id=1, source_target_pairs={{4,0},{8,4},{12,8},{0,12},{5,1},{9,5},{13,9},{1,13},{6,2},{10,6},{... | collective-permute-start | bytes 393224 | tf_op jit(solution)/shard_map/ppermute | solution.py:313
  133.3 4.3 %copy-start.8 = (bf16[3584]{0:T(1024)(128)(2,1)S(1)}, bf16[3584]{0:T(1024)(128)(2,1)}, u32[]{:S(2)}) copy-start(bf16[3584]{0:T(1024)(128)(2,1)} %param.17) | copy-start | bytes 21508
  133.3 1.9 %collective-permute-start.17 = (bf16[64,3584]{1,0:T(8,128)(2,1)S(1)}, bf16[64,3584]{1,0:T(8,128)(2,1)S(1)}, u32[]{:S(2)}, u32[]{:S(2)}) collective-permute-start(bf16[64,3584]{1,0:T(8,128)(2,1)S(1)} %get-tuple-element.8), channel_id=1, source_target_pairs={{0,1},{1,0},{2,3},{3,2},{4,5},{5,4},{6,7},{7,6},{8,9},{9,8},{10,11... | collective-permute-start | bytes 1376264 | tf_op jit(solution)/shard_map/ppermute | solution.py:304
  135.4 7.7 %collective-permute-start.18 = (bf16[32,3584]{1,0:T(8,128)(2,1)S(1)}, bf16[32,3584]{1,0:T(8,128)(2,1)S(1)}, u32[]{:S(2)}, u32[]{:S(2)}) collective-permute-start(bf16[32,3584]{1,0:T(8,128)(2,1)S(1)} %slice.91), channel_id=1, source_target_pairs={{2,0},{3,1},{0,2},{1,3},{6,4},{7,5},{4,6},{5,7},{10,8},{11,9},{8,1... | collective-permute-start | bytes 688136 | tf_op jit(solution)/shard_map/ppermute | solution.py:307

commit v2 on v0

v2 whole, which is shorter than its diff:
```python
import functools

import jax
import jax.numpy as jnp
import numpy as np
from jax import lax
from jax.experimental import pallas as pl
from jax.experimental.pallas import tpu as pltpu
from jax.sharding import PartitionSpec as P

HD = 256
HALF = HD // 2
PLEN = 512
QLEN = 64
CHUNKS = 4
TILE = 512
FLAG = 128
VMEM_LIMIT = 56 * 1024 * 1024
MESH = pl.DeviceIdType.MESH

epsilon = 1e-06
softcap_limit = 50.0


def tables(count):
    frequency = (10000.0 ** (-2.0 * np.arange(HALF, dtype=np.float32) / HD)).astype(np.float32)
    positions = np.arange(count, dtype=np.float32)
    angles = (positions[:, None] * frequency[None, :]).astype(np.float32)
    return jnp.asarray(np.stack([np.cos(angles), np.sin(angles)]))


def normalize(rows, gain):
    values = rows.astype(jnp.float32)
    inverse_rms = lax.rsqrt(jnp.mean(values * values, axis=-1, keepdims=True) + epsilon)
    return (values * inverse_rms * gain.astype(jnp.float32)).astype(jnp.bfloat16)


def turned(raw, cosine, sine):
    low, high = raw[:, :HALF], raw[:, HALF:]
    return jnp.concatenate([low * cosine - high * sine, high * cosine + low * sine], axis=1)


def capped_exp(scores):
    return jnp.exp(softcap_limit * jnp.tanh(scores / softcap_limit))


def columns(j, width):
    return pl.ds(pl.multiple_of(j * width, width), width)


def attend(pair_ref, held_ref, out_ref, heads_q, heads_kv, per_owner):
    groups = heads_q // heads_kv
    over = (((1,), (1,)), ((), ()))
    rows = lax.rem(lax.broadcasted_iota(jnp.int32, (groups * QLEN, QLEN), 0), QLEN)
    causal = rows >= lax.broadcasted_iota(jnp.int32, (groups * QLEN, QLEN), 1)
    flag_at = (heads_q + 2 * heads_kv) * HD
    flag = pair_ref[:, flag_at : flag_at + FLAG].astype(jnp.float32)[:, :1]
    flag = jnp.concatenate([flag] * groups, axis=0)
    for h in range(heads_kv):
        query = jnp.concatenate(
            [pair_ref[:, (h * groups + g) * HD : (h * groups + g + 1) * HD] for g in range(groups)],
            axis=0,
        )
        key_at, value_at = (heads_q + h) * HD, (heads_q + heads_kv + h) * HD
        keys_own = pair_ref[:, key_at : key_at + HD]
        values_own = pair_ref[:, value_at : value_at + HD]
        far = None
        for p in range(per_owner):
            keys = held_ref[p * PLEN : (p + 1) * PLEN, h * HD : (h + 1) * HD]
            scores = lax.dot_general(query, keys, over, preferred_element_type=jnp.float32)
            far = scores if p == 0 else jnp.where(flag == float(p), scores, far)
        far = capped_exp(far)
        near = capped_exp(
            lax.dot_general(query, keys_own, over, preferred_element_type=jnp.float32)
        )
        near = jnp.where(causal, near, 0.0)
        total = jnp.sum(far, axis=1, keepdims=True) + jnp.sum(near, axis=1, keepdims=True)
        far = far / total
        near = (near / total).astype(jnp.bfloat16)
        mixed = jnp.dot(near, values_own, preferred_element_type=jnp.float32)
        for p in range(per_owner):
            at = (heads_kv + h) * HD
            values = held_ref[p * PLEN : (p + 1) * PLEN, at : at + HD]
            weights = jnp.where(flag == float(p), far, 0.0).astype(jnp.bfloat16)
            mixed = mixed + jnp.dot(weights, values, preferred_element_type=jnp.float32)
        mixed = mixed.astype(jnp.bfloat16)
        for g in range(groups):
            at = (h * groups + g) * HD
            out_ref[:, at : at + HD] = mixed[g * QLEN : (g + 1) * QLEN]


def body(
    n_tp, n_dev,
    pairs_ref, count_ref, gain_in_ref, gain_out_ref, passage_ref, query_ref, table_ref,
    wq_ref, wk_ref, wv_ref, wo_ref, out_ref,
    raw, passage, held, gathered, suffix, turn, pack, received, mixed, returned, attended,
    wq, wk, wv, wo, work, product, keep, give, twin_in, sums, sums_in, merged,
    load_sem, raw_sem, query_send, query_recv, near_send, far_send, pass_send, rows_recv,
    pair_send, pair_recv, back_send, back_recv, give_send, give_recv, sum_send, sum_recv,
):
    n_chips = n_tp // 2
    lane, owner = lax.axis_index("tp"), lax.axis_index("dev")
    chip, core = lane // 2, lane % 2
    twin = chip * 2 + 1 - core
    heads_q, heads_kv = wq.shape[1] // HD, wk.shape[1] // HD
    block_rows, width = raw.shape
    unit = block_rows // CHUNKS
    size = query_ref.shape[0]
    per_owner = block_rows * n_tp // PLEN
    pair_slots = pairs_ref.shape[0]
    n_cols = width // TILE

    def peer(k):
        return lax.rem(chip + k, n_chips) * 2 + core

    def send(src, dst, send_sem, recv_sem, axis, target):
        copy = pltpu.make_async_remote_copy(
            src_ref=src, dst_ref=dst, send_sem=send_sem, recv_sem=recv_sem,
            device_id={axis: target}, device_id_type=MESH,
        )
        copy.start()

    def sent(ref, sem):
        pltpu.make_async_remote_copy(
            src_ref=ref, dst_ref=ref, send_sem=sem, recv_sem=sem,
            device_id={"tp": twin}, device_id_type=MESH,
        ).wait_send()

    def arrived(ref, sem):
        pltpu.make_async_remote_copy(
            src_ref=ref, dst_ref=ref, send_sem=sem, recv_sem=sem,
            device_id={"tp": twin}, device_id_type=MESH,
        ).wait_recv()

    def in_range(names, holder):
        return (names >= holder * per_owner) & (names < (holder + 1) * per_owner)

    for c in range(CHUNKS):
        at = pl.ds(c * unit, unit)
        pltpu.make_async_copy(passage_ref.at[at], raw.at[at], raw_sem.at[c]).start()
    loads = [
        pltpu.make_async_copy(query_ref, gathered.at[lane], load_sem.at[0]),
        pltpu.make_async_copy(table_ref, turn, load_sem.at[1]),
        pltpu.make_async_copy(wk_ref, wk, load_sem.at[2]),
        pltpu.make_async_copy(wv_ref, wv, load_sem.at[3]),
        pltpu.make_async_copy(wq_ref, wq, load_sem.at[4]),
        pltpu.make_async_copy(wo_ref, wo, load_sem.at[5]),
    ]
    for load in loads:
        load.start()

    barrier = pltpu.get_barrier_semaphore()
    pl.semaphore_signal(barrier, inc=1, device_id={"tp": twin}, device_id_type=MESH)
    for k in range(1, n_chips):
        pl.semaphore_signal(barrier, inc=1, device_id={"tp": peer(k)}, device_id_type=MESH)
    for k in range(1, n_dev):
        there = lax.rem(owner + k, n_dev)
        pl.semaphore_signal(barrier, inc=1, device_id={"dev": there}, device_id_type=MESH)
    pl.semaphore_wait(barrier, n_chips + n_dev - 1)

    for k in range(1, n_chips):
        send(query_ref, gathered.at[lane], query_send.at[k], query_recv.at[lane], "tp", peer(k))
    send(query_ref, gathered.at[lane], query_send.at[0], query_recv.at[lane], "tp", twin)

    def norm_chunk(c, carry):
        at = pl.ds(pl.multiple_of(c * unit, unit), unit)
        pltpu.make_async_copy(passage_ref.at[at], raw.at[at], raw_sem.at[c]).wait()
        passage[lane, at, :] = normalize(raw[at, :], gain_in_ref[...])
        mine = passage.at[lane, at]
        for k in range(1, n_chips):
            send(mine, mine, far_send.at[k - 1, c], rows_recv.at[lane, c], "tp", peer(k))
        send(mine, mine, near_send.at[c], rows_recv.at[lane, c], "tp", twin)
        return carry

    lax.fori_loop(0, CHUNKS, norm_chunk, 0)

    def project(block, first, rows):
        row = block * block_rows + first
        place = pl.multiple_of(row, rows)
        spot = pl.ds(pl.multiple_of(lax.rem(row, PLEN), rows), rows)

        def keys(j, carry):
            weights = wk[:, columns(j, HD)]
            product_ = jnp.dot(
                passage[block, pl.ds(first, rows), :], weights, preferred_element_type=jnp.float32
            )
            held[pl.ds(place, rows), columns(j, HD)] = turned(
                product_, turn[0, spot, :], turn[1, spot, :]
            ).astype(jnp.bfloat16)
            return carry

        def values(j, carry):
            weights = wv[:, columns(j, HD)]
            product_ = jnp.dot(
                passage[block, pl.ds(first, rows), :], weights, preferred_element_type=jnp.float32
            )
            held[pl.ds(place, rows), columns(heads_kv + j, HD)] = product_.astype(jnp.bfloat16)
            return carry

        lax.fori_loop(0, heads_kv, keys, 0)
        lax.fori_loop(0, heads_kv, values, 0)

    for load in loads[1:4]:
        load.wait()
    project(lane, 0, block_rows)

    for k in range(1, n_chips):
        arrived(gathered.at[peer(k)], query_recv.at[peer(k)])
        block = gathered.at[peer(k)]
        send(block, block, query_send.at[n_chips + k - 1], query_recv.at[peer(k)], "tp", twin)
    arrived(gathered.at[twin], query_recv.at[twin])
    for k in range(1, n_chips):
        other = lax.rem(chip + k, n_chips) * 2 + 1 - core
        arrived(gathered.at[other], query_recv.at[other])
    loads[0].wait()
    for i in range(n_tp):
        suffix[i * size : (i + 1) * size, :] = normalize(gathered[i], gain_in_ref[...])
    flag_at = (heads_q + 2 * heads_kv) * HD
    for k in range(n_dev):
        there = lax.rem(owner + k, n_dev)
        name = jnp.full((QLEN, FLAG), pairs_ref[0])
        for s in range(1, pair_slots):
            other = jnp.full((QLEN, FLAG), pairs_ref[s])
            name = jnp.where(in_range(other, there), other, name)
        flag = jnp.zeros((QLEN, FLAG), jnp.float32)
        for p in range(1, per_owner):
            for o in range(n_dev):
                flag = jnp.where(name == o * per_owner + p, float(p), flag)
        pack[k, :, flag_at : flag_at + FLAG] = flag.astype(jnp.bfloat16)
    loads[4].wait()

    def store(j):
        for k in range(n_dev):
            there = lax.rem(owner + k, n_dev)
            rows = work[:QLEN, :]
            for s in range(1, pair_slots):
                hit = in_range(jnp.full((QLEN, HD), pairs_ref[s]), there)
                rows = jnp.where(hit, work[s * QLEN : (s + 1) * QLEN, :], rows)
            pack[k, :, columns(j, HD)] = rows.astype(jnp.bfloat16)

    def spun(values):
        cosine = jnp.concatenate([turn[0, PLEN : PLEN + QLEN, :]] * pair_slots, axis=0)
        sine = jnp.concatenate([turn[1, PLEN : PLEN + QLEN, :]] * pair_slots, axis=0)
        return turned(values, cosine, sine)

    def suffix_queries(j, carry):
        raw_ = jnp.dot(suffix[...], wq[:, columns(j, HD)], preferred_element_type=jnp.float32)
        work[...] = spun(raw_) * HD ** (-0.5)
        store(j)
        return carry

    def suffix_keys(j, carry):
        raw_ = jnp.dot(suffix[...], wk[:, columns(j, HD)], preferred_element_type=jnp.float32)
        work[...] = spun(raw_)
        store(heads_q + j)
        return carry

    def suffix_values(j, carry):
        work[...] = jnp.dot(suffix[...], wv[:, columns(j, HD)], preferred_element_type=jnp.float32)
        store(heads_q + heads_kv + j)
        return carry

    lax.fori_loop(0, heads_q, suffix_queries, 0)
    lax.fori_loop(0, heads_kv, suffix_keys, 0)
    lax.fori_loop(0, heads_kv, suffix_values, 0)
    for k in range(1, n_dev):
        there = lax.rem(owner + k, n_dev)
        send(pack.at[k], received.at[k - 1], pair_send.at[k - 1], pair_recv.at[k - 1], "dev", there)

    for c in range(CHUNKS):
        at = pl.ds(c * unit, unit)
        arrived(passage.at[twin, at], rows_recv.at[twin, c])
    project(twin, 0, block_rows)
    for k in range(1, n_chips):
        here = peer(k)
        other = lax.rem(chip + k, n_chips) * 2 + 1 - core

        def step(i, carry):
            for half in range(2):
                c = i * 2 + half
                rows = passage.at[here, pl.ds(pl.multiple_of(c * unit, unit), unit)]
                arrived(rows, rows_recv.at[here, c])
                send(rows, rows, pass_send.at[k - 1, c], rows_recv.at[here, c], "tp", twin)
            first = pl.multiple_of(i * 2 * unit, 2 * unit)
            project(here, first, 2 * unit)
            for half in range(2):
                c = i * 2 + half
                rows = passage.at[other, pl.ds(pl.multiple_of(c * unit, unit), unit)]
                arrived(rows, rows_recv.at[other, c])
            project(other, first, 2 * unit)
            return carry

        lax.fori_loop(0, CHUNKS // 2, step, 0)

    def pair_step(i, carry):
        arrived(received.at[i], pair_recv.at[i])
        attend(received.at[i], held, mixed.at[i], heads_q, heads_kv, per_owner)
        back = lax.rem(owner + n_dev - 1 - i, n_dev)
        send(mixed.at[i], returned.at[i + 1], back_send.at[i], back_recv.at[i], "dev", back)
        return carry

    lax.fori_loop(0, n_dev - 1, pair_step, 0)
    attend(pack.at[0], held, returned.at[0], heads_q, heads_kv, per_owner)
    loads[5].wait()
    for i in range(n_dev - 1):
        arrived(returned.at[i + 1], back_recv.at[i])
    for s in range(pair_slots):
        name = jnp.full(returned.shape[1:], pairs_ref[s])
        rows = returned[0].astype(jnp.float32)
        for k in range(1, n_dev):
            there = lax.rem(owner + k, n_dev)
            rows = jnp.where(in_range(name, there), returned[k].astype(jnp.float32), rows)
        attended[s * QLEN : (s + 1) * QLEN, :] = rows.astype(jnp.bfloat16)

    def pass_on(j):
        arrived(twin_in.at[j], give_recv.at[j])
        summed = keep[j].astype(jnp.float32) + twin_in[j].astype(jnp.float32)
        merged[j] = summed[:size]
        for k in range(1, n_chips):
            sums[k - 1, j] = summed[k * size : (k + 1) * size].astype(jnp.bfloat16)
            send(
                sums.at[k - 1, j], sums_in.at[k - 1, j],
                sum_send.at[k - 1, j], sum_recv.at[k - 1, j], "tp", peer(k),
            )

    def out_step(j, carry):
        product[...] = jnp.dot(
            attended[...], wo[:, columns(j, TILE)], preferred_element_type=jnp.float32
        )
        for k in range(n_chips):
            base = lax.rem(chip + k, n_chips) * 2
            mine = pl.multiple_of((base + core) * size, size)
            theirs = pl.multiple_of((base + 1 - core) * size, size)
            at = pl.ds(k * size, size)
            keep[j, at, :] = product[pl.ds(mine, size), :].astype(jnp.bfloat16)
            give[j, at, :] = product[pl.ds(theirs, size), :].astype(jnp.bfloat16)
        send(give.at[j], twin_in.at[j], give_send.at[j], give_recv.at[j], "tp", twin)

        @pl.when(j > 0)
        def _():
            pass_on(j - 1)

        return carry

    lax.fori_loop(0, n_cols, out_step, 0)
    pass_on(n_cols - 1)
    squares = jnp.zeros((size, 1), jnp.float32)
    for j in range(n_cols):
        total = merged[j]
        for k in range(1, n_chips):
            arrived(sums_in.at[k - 1, j], sum_recv.at[k - 1, j])
            total = total + sums_in[k - 1, j].astype(jnp.float32)
        merged[j] = total
        squares = squares + jnp.sum(total * total, axis=1, keepdims=True)
    scale = lax.rsqrt(squares / width + epsilon)
    row_ids = lane * size + lax.broadcasted_iota(jnp.int32, (size, TILE), 0)
    alive = row_ids < count_ref[0] * QLEN
    for j in range(n_cols):
        at = slice(j * TILE, (j + 1) * TILE)
        branch = merged[j] * scale * gain_out_ref[:, at].astype(jnp.float32)
        whole = gathered[lane, :, at].astype(jnp.float32) + branch
        out_ref[:, at] = jnp.where(alive, whole, 0.0).astype(jnp.bfloat16)

    for k in range(2 * n_chips - 1):
        sent(gathered.at[0], query_send.at[k])
    for c in range(CHUNKS):
        rows = passage.at[0, pl.ds(0, unit)]
        sent(rows, near_send.at[c])
        for k in range(n_chips - 1):
            sent(rows, far_send.at[k, c])
            sent(rows, pass_send.at[k, c])
    for i in range(n_dev - 1):
        sent(received.at[i], pair_send.at[i])
        sent(mixed.at[i], back_send.at[i])
    for j in range(n_cols):
        sent(give.at[j], give_send.at[j])
        for k in range(n_chips - 1):
            sent(sums.at[k, j], sum_send.at[k, j])


def shards(
    passage_hidden,
    query_hidden,
    gain_in,
    gain_out,
    w_query,
    w_key,
    w_value,
    w_out,
    pair_passage,
    pair_count,
):
    n_tp, n_dev = lax.axis_size("tp"), lax.axis_size("dev")
    n_chips = n_tp // 2
    pair_slots = pair_passage.shape[0]
    block_rows, width = passage_hidden.shape
    size = query_hidden.shape[0]
    rows = pair_slots * QLEN
    wide_q, wide_kv = w_query.shape[1], w_key.shape[1]
    pack_width = wide_q + 2 * wide_kv + FLAG
    n_cols = width // TILE
    half = rows // 2
    bf, f32, dma = jnp.bfloat16, jnp.float32, pltpu.SemaphoreType.DMA
    smem = pl.BlockSpec(memory_space=pltpu.SMEM)
    vmem = pl.BlockSpec(memory_space=pltpu.VMEM)
    hbm = pl.BlockSpec(memory_space=pl.ANY)
    far = n_chips - 1
    return pl.pallas_call(
        functools.partial(body, n_tp, n_dev),
        out_shape=jax.ShapeDtypeStruct((size, width), bf),
        in_specs=[smem, smem, vmem, vmem] + [hbm] * 7,
        out_specs=vmem,
        scratch_shapes=[
            pltpu.VMEM((block_rows, width), bf),
            pltpu.VMEM((n_tp, block_rows, width), bf),
            pltpu.VMEM((n_tp * block_rows, 2 * wide_kv), bf),
            pltpu.VMEM((n_tp, size, width), bf),
            pltpu.VMEM((rows, width), bf),
            pltpu.VMEM((2, PLEN + QLEN, HALF), f32),
            pltpu.VMEM((n_dev, QLEN, pack_width), bf),
            pltpu.VMEM((n_dev - 1, QLEN, pack_width), bf),
            pltpu.VMEM((n_dev - 1, QLEN, wide_q), bf),
            pltpu.VMEM((n_dev, QLEN, wide_q), bf),
            pltpu.VMEM((rows, wide_q), bf),
            pltpu.VMEM(w_query.shape, bf),
            pltpu.VMEM(w_key.shape, bf),
            pltpu.VMEM(w_value.shape, bf),
            pltpu.VMEM(w_out.shape, bf),
            pltpu.VMEM((rows, HD), f32),
            pltpu.VMEM((rows, TILE), f32),
            pltpu.VMEM((n_cols, half, TILE), bf),
            pltpu.VMEM((n_cols, half, TILE), bf),
            pltpu.VMEM((n_cols, half, TILE), bf),
            pltpu.VMEM((far, n_cols, size, TILE), bf),
            pltpu.VMEM((far, n_cols, size, TILE), bf),
            pltpu.VMEM((n_cols, size, TILE), f32),
            dma((6,)),
            dma((CHUNKS,)),
            dma((2 * n_chips - 1,)),
            dma((n_tp,)),
            dma((CHUNKS,)),
            dma((far, CHUNKS)),
            dma((far, CHUNKS)),
            dma((n_tp, CHUNKS)),
            dma((n_dev - 1,)),
            dma((n_dev - 1,)),
            dma((n_dev - 1,)),
            dma((n_dev - 1,)),
            dma((n_cols,)),
            dma((n_cols,)),
            dma((far, n_cols)),
            dma((far, n_cols)),
        ],
        compiler_params=pltpu.CompilerParams(
            collective_id=0, has_side_effects=True, vmem_limit_bytes=VMEM_LIMIT
        ),
    )(
        pair_passage,
        pair_count,
        gain_in.reshape(1, width),
        gain_out.reshape(1, width),
        passage_hidden,
        query_hidden,
        tables(PLEN + QLEN),
        w_query,
        w_key,
        w_value,
        w_out,
    )


def solution(mesh):
    placed = (
        P(("grp", "dev", "tp"), None),
        P(("grp", "dev", "tp"), None),
        P(),
        P(),
        P(None, "tp"),
        P(None, "tp"),
        P(None, "tp"),
        P("tp", None),
        P(("grp", "dev")),
        P(("grp", "dev")),
    )
    return jax.shard_map(
        shards, mesh=mesh, in_specs=placed, out_specs=P(("grp", "dev", "tp"), None), check_vma=False
    )
```

time: 288 us -> 84.5 us (0.29)
  waiting for transfers between devices: 203 us -> 0 us
  Pallas kernels: 0 us -> 79.2 us
  matrix products: 35.3 us -> 0 us
  between operations: 14.1 us -> 0.66 us
  other arithmetic: 13.2 us -> 0 us
  blocking collectives: 9.35 us -> 0 us
  local copies, waits for them, and re-layouts: 12 us -> 4.26 us
    all_gather x2 -> x0, waiting for transfers between devices: 181 us -> none  [the longest x1 127 us: shards(): fetched = lax.all_gather(prepared, 'dev', axis=0, tiled=True)]
    pallas_call x0 -> x1, Pallas kernels: none -> 79.2 us  [shards(): pl.pallas_call(functools.partial(body, n_tp, n_dev), out_shape=jax.ShapeD...]
    dot_general x10 -> x0, matrix products: 35.3 us -> none  [the longest x2 10.9 us: shards(): values = jnp.dot(normed, w_value, preferred_element_type=jnp.float32)]
    reduce_scatter x1 -> x0, waiting for transfers between devices: 21.7 us -> none  [shards(): lax.psum_scatter(settle(jnp.dot(attended, w_out, preferred_element_type=j...]
    all_gather x1 -> x0, blocking collectives: 9.35 us -> none  [shards(): segment = lax.all_gather(query_hidden, 'tp', axis=0, tiled=True)]
    reduce_sum x3 -> x0, other arithmetic: 6.08 us -> none  [the longest x2 4.99 us: normalize(): jnp.mean(values * values, axis=-1, keepdims=True) + epsilon]
    gather x1 -> x0, local copies, waits for them, and re-layouts: 4.06 us -> none  [one_pair(): lax.dynamic_index_in_dim(fetched, passage_row, 0, keepdims=False)]
    slice x5 -> x0, local copies, waits for them, and re-layouts: 3.43 us -> none  [the longest x2 1.72 us: attend(): far_block[:, heads_kv * head_width:].reshape(-1, heads_kv, head_width)]
  transfers between devices with their start and end apart: 3 -> 0, of which waited for: 3 -> 0; matrix products, arithmetic and copies ran while one was open for 5% -> 0% of each run, Pallas kernels for 0% -> 0%
where the time goes in v2:
time: 84.5 us; the launch traced here: 84.1 us
  Pallas kernels  79.2 us (94%)
  local copies, waits for them, and re-layouts  4.26 us (5%)
    pallas_call x1, Pallas kernels, shards(): pl.pallas_call(functools.partial(body, n_tp, n_dev), out_shape=jax.ShapeD...  79.2 us

profile of v2, /device:TPU:0, one launch (start us, length us, event | category | flops | bytes accessed | tf_op | source)
XLA Modules:
  0.0 84.1 jit_solution(10249226805345045254)
XLA Ops:
  0.7 1.3 %reshape.6.gain_in_ref = bf16[1,3584]{1,0:T(2,128)(2,1)} reshape(bf16[3584]{0:T(1024)(128)(2,1)} %param.13) | data formatting | bytes 14336 | tf_op jit(solution)/shard_map/reshape | solution.py:460
  2.0 1.3 %reshape.7.gain_out_ref = bf16[1,3584]{1,0:T(2,128)(2,1)} reshape(bf16[3584]{0:T(1024)(128)(2,1)} %param.14) | data formatting | bytes 14336 | tf_op jit(solution)/shard_map/reshape | solution.py:461
  3.3 79.2 %shard_map.109 = bf16[32,3584]{1,0:T(8,128)(2,1)} custom-call(s32[2]{0:T(128)} %pairs_ref.1, s32[1]{0:T(128)S(6)} %copy.13.count_ref, bf16[1,3584]{1,0:T(2,128)(2,1)} %reshape.6.gain_in_ref, bf16[1,3584]{1,0:T(2,128)(2,1)} %reshape.7.gain_out_ref, bf16[256,3584]{1,0:T(8,128)(2,1)} %passage_ref.1, bf16[32,3584]{1,0:T(8,128)(2,1)} %query_ref.1, ...), custom_call_target="tpu_custom_call" | custom-call | tf_op jit(solution)/shard_map/pallas_call | solution.py:408
  82.5 1.6 %copy.14 = bf16[32,3584]{1,0:T(8,128)(2,1)} copy(bf16[32,3584]{1,0:T(8,128)(2,1)} %shard_map.109) | data formatting | bytes 458752

commit v3 on v2

--- a/solution.py
+++ b/solution.py
@@ -32,7 +32,7 @@
 def normalize(rows, gain):
     values = rows.astype(jnp.float32)
     inverse_rms = lax.rsqrt(jnp.mean(values * values, axis=-1, keepdims=True) + epsilon)
-    return (values * inverse_rms * gain.astype(jnp.float32)).astype(jnp.bfloat16)
+    return (values * inverse_rms * gain).astype(jnp.bfloat16)
 
 
 def turned(raw, cosine, sine):
@@ -41,14 +41,14 @@
 
 
 def capped_exp(scores):
-    return jnp.exp(softcap_limit * jnp.tanh(scores / softcap_limit))
+    return jnp.exp(softcap_limit * jnp.tanh(scores * (1.0 / softcap_limit)))
 
 
 def columns(j, width):
     return pl.ds(pl.multiple_of(j * width, width), width)
 
 
-def attend(pair_ref, held_ref, out_ref, heads_q, heads_kv, per_owner):
+def attend(pair_ref, held_ref, out_ref, heads_q, heads_kv, passages, other_ref=None):
     groups = heads_q // heads_kv
     over = (((1,), (1,)), ((), ()))
     rows = lax.rem(lax.broadcasted_iota(jnp.int32, (groups * QLEN, QLEN), 0), QLEN)
@@ -65,35 +65,40 @@
         keys_own = pair_ref[:, key_at : key_at + HD]
         values_own = pair_ref[:, value_at : value_at + HD]
         far = None
-        for p in range(per_owner):
-            keys = held_ref[p * PLEN : (p + 1) * PLEN, h * HD : (h + 1) * HD]
+        for i, p in enumerate(passages):
+            keys = held_ref[columns(p, PLEN), h * HD : (h + 1) * HD]
             scores = lax.dot_general(query, keys, over, preferred_element_type=jnp.float32)
-            far = scores if p == 0 else jnp.where(flag == float(p), scores, far)
+            far = scores if i == 0 else jnp.where(flag == jnp.float32(p), scores, far)
         far = capped_exp(far)
         near = capped_exp(
             lax.dot_general(query, keys_own, over, preferred_element_type=jnp.float32)
         )
         near = jnp.where(causal, near, 0.0)
         total = jnp.sum(far, axis=1, keepdims=True) + jnp.sum(near, axis=1, keepdims=True)
-        far = far / total
-        near = (near / total).astype(jnp.bfloat16)
+        inverse = 1.0 / total
+        far = far * inverse
+        near = (near * inverse).astype(jnp.bfloat16)
         mixed = jnp.dot(near, values_own, preferred_element_type=jnp.float32)
-        for p in range(per_owner):
+        for p in passages:
             at = (heads_kv + h) * HD
-            values = held_ref[p * PLEN : (p + 1) * PLEN, at : at + HD]
-            weights = jnp.where(flag == float(p), far, 0.0).astype(jnp.bfloat16)
+            values = held_ref[columns(p, PLEN), at : at + HD]
+            weights = far if len(passages) == 1 else jnp.where(flag == jnp.float32(p), far, 0.0)
+            weights = weights.astype(jnp.bfloat16)
             mixed = mixed + jnp.dot(weights, values, preferred_element_type=jnp.float32)
-        mixed = mixed.astype(jnp.bfloat16)
         for g in range(groups):
             at = (h * groups + g) * HD
-            out_ref[:, at : at + HD] = mixed[g * QLEN : (g + 1) * QLEN]
+            part = mixed[g * QLEN : (g + 1) * QLEN]
+            if other_ref is not None:
+                chosen = flag[:QLEN] == passages[0].astype(jnp.float32)
+                part = jnp.where(chosen, part, other_ref[:, at : at + HD].astype(jnp.float32))
+            out_ref[:, at : at + HD] = part.astype(jnp.bfloat16)
 
 
 def body(
     n_tp, n_dev,
     pairs_ref, count_ref, gain_in_ref, gain_out_ref, passage_ref, query_ref, table_ref,
     wq_ref, wk_ref, wv_ref, wo_ref, out_ref,
-    raw, passage, held, gathered, suffix, turn, pack, received, mixed, returned, attended,
+    raw, passage, held, gathered, suffix, turn, pack, received, mixed, early, returned, attended,
     wq, wk, wv, wo, work, product, keep, give, twin_in, sums, sums_in, merged,
     load_sem, raw_sem, query_send, query_recv, near_send, far_send, pass_send, rows_recv,
     pair_send, pair_recv, back_send, back_recv, give_send, give_recv, sum_send, sum_recv,
@@ -109,6 +114,7 @@
     per_owner = block_rows * n_tp // PLEN
     pair_slots = pairs_ref.shape[0]
     n_cols = width // TILE
+    halves = n_chips == 2 and per_owner == 2
 
     def peer(k):
         return lax.rem(chip + k, n_chips) * 2 + core
@@ -165,7 +171,7 @@
     def norm_chunk(c, carry):
         at = pl.ds(pl.multiple_of(c * unit, unit), unit)
         pltpu.make_async_copy(passage_ref.at[at], raw.at[at], raw_sem.at[c]).wait()
-        passage[lane, at, :] = normalize(raw[at, :], gain_in_ref[...])
+        passage[lane, at, :] = normalize(raw[at, :], gain_in_ref[...].astype(jnp.float32).reshape(1, width))
         mine = passage.at[lane, at]
         for k in range(1, n_chips):
             send(mine, mine, far_send.at[k - 1, c], rows_recv.at[lane, c], "tp", peer(k))
@@ -214,7 +220,7 @@
         arrived(gathered.at[other], query_recv.at[other])
     loads[0].wait()
     for i in range(n_tp):
-        suffix[i * size : (i + 1) * size, :] = normalize(gathered[i], gain_in_ref[...])
+        suffix[i * size : (i + 1) * size, :] = normalize(gathered[i], gain_in_ref[...].astype(jnp.float32).reshape(1, width))
     flag_at = (heads_q + 2 * heads_kv) * HD
     for k in range(n_dev):
         there = lax.rem(owner + k, n_dev)
@@ -275,32 +281,50 @@
         here = peer(k)
         other = lax.rem(chip + k, n_chips) * 2 + 1 - core
 
-        def step(i, carry):
-            for half in range(2):
-                c = i * 2 + half
+        def step(many, i, carry):
+            for part in range(many):
+                c = i * many + part
                 rows = passage.at[here, pl.ds(pl.multiple_of(c * unit, unit), unit)]
                 arrived(rows, rows_recv.at[here, c])
                 send(rows, rows, pass_send.at[k - 1, c], rows_recv.at[here, c], "tp", twin)
-            first = pl.multiple_of(i * 2 * unit, 2 * unit)
-            project(here, first, 2 * unit)
-            for half in range(2):
-                c = i * 2 + half
+            first = pl.multiple_of(i * many * unit, many * unit)
+            project(here, first, many * unit)
+            for part in range(many):
+                c = i * many + part
                 rows = passage.at[other, pl.ds(pl.multiple_of(c * unit, unit), unit)]
                 arrived(rows, rows_recv.at[other, c])
-            project(other, first, 2 * unit)
+            project(other, first, many * unit)
             return carry
 
-        lax.fori_loop(0, CHUNKS // 2, step, 0)
+        lax.fori_loop(0, CHUNKS // 2 - 1, functools.partial(step, 2), 0)
+        if halves:
+            lax.fori_loop(CHUNKS - 2, CHUNKS - 1, functools.partial(step, 1), 0)
+
+            def early_step(i, carry):
+                arrived(received.at[i], pair_recv.at[i])
+                attend(received.at[i], held, early.at[i + 1], heads_q, heads_kv, [chip])
+                return carry
+
+            attend(pack.at[0], held, early.at[0], heads_q, heads_kv, [chip])
+            lax.fori_loop(0, n_dev - 1, early_step, 0)
+            lax.fori_loop(CHUNKS - 1, CHUNKS, functools.partial(step, 1), 0)
+        else:
+            lax.fori_loop(CHUNKS - 2, CHUNKS, functools.partial(step, 1), 0)
+
+    passages = [1 - chip] if halves else list(range(per_owner))
 
     def pair_step(i, carry):
-        arrived(received.at[i], pair_recv.at[i])
-        attend(received.at[i], held, mixed.at[i], heads_q, heads_kv, per_owner)
+        if not halves:
+            arrived(received.at[i], pair_recv.at[i])
+        other = early.at[i + 1] if halves else None
+        attend(received.at[i], held, mixed.at[i], heads_q, heads_kv, passages, other)
         back = lax.rem(owner + n_dev - 1 - i, n_dev)
         send(mixed.at[i], returned.at[i + 1], back_send.at[i], back_recv.at[i], "dev", back)
         return carry
 
     lax.fori_loop(0, n_dev - 1, pair_step, 0)
-    attend(pack.at[0], held, returned.at[0], heads_q, heads_kv, per_owner)
+    other = early.at[0] if halves else None
+    attend(pack.at[0], held, returned.at[0], heads_q, heads_kv, passages, other)
     loads[5].wait()
     for i in range(n_dev - 1):
         arrived(returned.at[i + 1], back_recv.at[i])
@@ -357,7 +381,7 @@
     alive = row_ids < count_ref[0] * QLEN
     for j in range(n_cols):
         at = slice(j * TILE, (j + 1) * TILE)
-        branch = merged[j] * scale * gain_out_ref[:, at].astype(jnp.float32)
+        branch = merged[j] * scale * gain_out_ref[at].astype(jnp.float32).reshape(1, TILE)
         whole = gathered[lane, :, at].astype(jnp.float32) + branch
         out_ref[:, at] = jnp.where(alive, whole, 0.0).astype(jnp.bfloat16)
 
@@ -421,6 +445,7 @@
             pltpu.VMEM((n_dev - 1, QLEN, pack_width), bf),
             pltpu.VMEM((n_dev - 1, QLEN, wide_q), bf),
             pltpu.VMEM((n_dev, QLEN, wide_q), bf),
+            pltpu.VMEM((n_dev, QLEN, wide_q), bf),
             pltpu.VMEM((rows, wide_q), bf),
             pltpu.VMEM(w_query.shape, bf),
             pltpu.VMEM(w_key.shape, bf),
@@ -457,8 +482,8 @@
     )(
         pair_passage,
         pair_count,
-        gain_in.reshape(1, width),
-        gain_out.reshape(1, width),
+        gain_in,
+        gain_out,
         passage_hidden,
         query_hidden,
         tables(PLEN + QLEN),

time: 84.5 us -> 81.6 us (0.966)
  local copies, waits for them, and re-layouts: 4.26 us -> 1.64 us
    reshape x2 -> x0, local copies, waits for them, and re-layouts: 2.62 us -> none  [the longest x1 1.31 us: shards(): gain_out.reshape(1, width)]
where the time goes in v3:
time: 81.6 us; the launch traced here: 81.4 us
  Pallas kernels  79.1 us (97%)
  local copies, waits for them, and re-layouts  1.64 us (2%)
    pallas_call x1, Pallas kernels, shards(): pl.pallas_call(functools.partial(body, n_tp, n_dev), out_shape=jax.ShapeD...  79.1 us
    unnamed x1, local copies, waits for them, and re-layouts  1.64 us

profile of v3, /device:TPU:0, one launch (start us, length us, event | category | flops | bytes accessed | tf_op | source)
XLA Modules:
  0.0 81.4 jit_solution(1396856056344449669)
XLA Ops:
  0.7 79.1 %shard_map.109 = bf16[32,3584]{1,0:T(8,128)(2,1)} custom-call(s32[2]{0:T(128)} %pairs_ref.1, s32[1]{0:T(128)S(6)} %copy.13.count_ref, bf16[3584]{0:T(1024)(128)(2,1)} %gain_in_ref.1, bf16[3584]{0:T(1024)(128)(2,1)} %gain_out_ref.1, bf16[256,3584]{1,0:T(8,128)(2,1)} %passage_ref.1, bf16[32,3584]{1,0:T(8,128)(2,1)} %query_ref.1, ...), custom_call_target="tpu_custom_call" | custom-call | tf_op jit(solution)/shard_map/pallas_call | solution.py:432
  79.7 1.6 %copy.14 = bf16[32,3584]{1,0:T(8,128)(2,1)} copy(bf16[32,3584]{1,0:T(8,128)(2,1)} %shard_map.109) | data formatting | bytes 458752

commit v4 on v3

--- a/solution.py
+++ b/solution.py
@@ -180,27 +180,26 @@
 
     lax.fori_loop(0, CHUNKS, norm_chunk, 0)
 
-    def project(block, first, rows):
-        row = block * block_rows + first
-        place = pl.multiple_of(row, rows)
-        spot = pl.ds(pl.multiple_of(lax.rem(row, PLEN), rows), rows)
+    def project(blocks, first, rows):
+        def product_of(weights):
+            parts = [passage[block, pl.ds(first, rows), :] for block in blocks]
+            whole = parts[0] if len(parts) == 1 else jnp.concatenate(parts, axis=0)
+            whole = jnp.dot(whole, weights, preferred_element_type=jnp.float32)
+            return [whole[n * rows : (n + 1) * rows] for n in range(len(blocks))]
 
         def keys(j, carry):
-            weights = wk[:, columns(j, HD)]
-            product_ = jnp.dot(
-                passage[block, pl.ds(first, rows), :], weights, preferred_element_type=jnp.float32
-            )
-            held[pl.ds(place, rows), columns(j, HD)] = turned(
-                product_, turn[0, spot, :], turn[1, spot, :]
-            ).astype(jnp.bfloat16)
+            for block, part in zip(blocks, product_of(wk[:, columns(j, HD)])):
+                row = block * block_rows + first
+                spot = pl.ds(pl.multiple_of(lax.rem(row, PLEN), rows), rows)
+                held[pl.ds(pl.multiple_of(row, rows), rows), columns(j, HD)] = turned(
+                    part, turn[0, spot, :], turn[1, spot, :]
+                ).astype(jnp.bfloat16)
             return carry
 
         def values(j, carry):
-            weights = wv[:, columns(j, HD)]
-            product_ = jnp.dot(
-                passage[block, pl.ds(first, rows), :], weights, preferred_element_type=jnp.float32
-            )
-            held[pl.ds(place, rows), columns(heads_kv + j, HD)] = product_.astype(jnp.bfloat16)
+            for block, part in zip(blocks, product_of(wv[:, columns(j, HD)])):
+                place = pl.ds(pl.multiple_of(block * block_rows + first, rows), rows)
+                held[place, columns(heads_kv + j, HD)] = part.astype(jnp.bfloat16)
             return carry
 
         lax.fori_loop(0, heads_kv, keys, 0)
@@ -208,7 +207,7 @@
 
     for load in loads[1:4]:
         load.wait()
-    project(lane, 0, block_rows)
+    project([lane], 0, block_rows)
 
     for k in range(1, n_chips):
         arrived(gathered.at[peer(k)], query_recv.at[peer(k)])
@@ -276,7 +275,7 @@
     for c in range(CHUNKS):
         at = pl.ds(c * unit, unit)
         arrived(passage.at[twin, at], rows_recv.at[twin, c])
-    project(twin, 0, block_rows)
+    project([twin], 0, block_rows)
     for k in range(1, n_chips):
         here = peer(k)
         other = lax.rem(chip + k, n_chips) * 2 + 1 - core
@@ -288,12 +287,11 @@
                 arrived(rows, rows_recv.at[here, c])
                 send(rows, rows, pass_send.at[k - 1, c], rows_recv.at[here, c], "tp", twin)
             first = pl.multiple_of(i * many * unit, many * unit)
-            project(here, first, many * unit)
             for part in range(many):
                 c = i * many + part
                 rows = passage.at[other, pl.ds(pl.multiple_of(c * unit, unit), unit)]
                 arrived(rows, rows_recv.at[other, c])
-            project(other, first, many * unit)
+            project([here, other], first, many * unit)
             return carry
 
         lax.fori_loop(0, CHUNKS // 2 - 1, functools.partial(step, 2), 0)

time: 81.6 us -> 80.2 us (0.983)
  Pallas kernels: 79.1 us -> 77.7 us
    pallas_call x1, Pallas kernels: 79.1 us -> 77.7 us  [shards(): pl.pallas_call(functools.partial(body, n_tp, n_dev), out_shape=jax.ShapeD...]
where the time goes in v4:
time: 80.2 us; the launch traced here: 80 us
  Pallas kernels  77.7 us (97%)
  local copies, waits for them, and re-layouts  1.64 us (2%)
    pallas_call x1, Pallas kernels, shards(): pl.pallas_call(functools.partial(body, n_tp, n_dev), out_shape=jax.ShapeD...  77.7 us
    unnamed x1, local copies, waits for them, and re-layouts  1.64 us

profile of v4, /device:TPU:0, one launch (start us, length us, event | category | flops | bytes accessed | tf_op | source)
XLA Modules:
  0.0 80.0 jit_solution(1729304271055099773)
XLA Ops:
  0.7 77.7 %shard_map.109 = bf16[32,3584]{1,0:T(8,128)(2,1)} custom-call(s32[2]{0:T(128)} %pairs_ref.1, s32[1]{0:T(128)S(6)} %copy.13.count_ref, bf16[3584]{0:T(1024)(128)(2,1)} %gain_in_ref.1, bf16[3584]{0:T(1024)(128)(2,1)} %gain_out_ref.1, bf16[256,3584]{1,0:T(8,128)(2,1)} %passage_ref.1, bf16[32,3584]{1,0:T(8,128)(2,1)} %query_ref.1, ...), custom_call_target="tpu_custom_call" | custom-call | tf_op jit(solution)/shard_map/pallas_call | solution.py:430
  78.4 1.6 %copy.14 = bf16[32,3584]{1,0:T(8,128)(2,1)} copy(bf16[32,3584]{1,0:T(8,128)(2,1)} %shard_map.109) | data formatting | bytes 458752
